TPU v7x, 32 devices: a whole 2x2x4 slice. The times are simulated.
32 devices in a mesh: ctx: 8 (over z, x), ch: 4 (over y, core).
Axes of the slice: x: 2, y: 2, z: 4, core: 2. Of those that a mesh axis runs over, the one named last changes fastest.
Arguments:
- streams: bfloat16 [3, 8192, 2048], P(None, ('ch', 'ctx')), may hold values from -6 to 6
- short_taps: float32 [3, 512, 7], P(None, 'ch'), may hold values from -3 to 3
- pole_rates: float32 [512, 16], P('ch'), may hold values from 2.4414063e-05 to 0.2, as said below
- residues: float32 [512, 16], P('ch'), may hold values from -0.6 to 0.6
- skip: float32 [8192], P('ch'), may hold values from -1 to 1
- gain: float32 [8192], P('ch'), may hold values from 0.1 to 1.9
Outputs:
- normed: bfloat16 [8192, 2048], P('ch', 'ctx')
Inputs may be any that keep to these rules, and one draw needn't show every extreme that they name: `pole_rates`: decay rates, all positive.
All inputs are finite; a program needn't handle non-finite values.
Results may differ from a plain program's by a relative error of at most 0.001.
Values may be sent and summed in bfloat16 or wider, within the bound.
A program may use at most 128 MiB of HBM per device.

v0:
```python
import jax
import jax.numpy as jnp
from jax import lax
from jax.sharding import PartitionSpec as P

D = 8192
SHORT = 7
BLOCK = 128


HIGHEST_PRECISION = lax.Precision.HIGHEST


def passed_along(array, axis, by):
    count = lax.axis_size(axis)
    pairs = [(i, i + by) for i in range(count) if 0 <= i + by < count]
    return lax.ppermute(array, axis, pairs)


def short_filter(extended, short_taps, groups, length):
    reach_back = short_taps.shape[2] - 1
    channels = extended.shape[1]
    shaped = extended.reshape(3, groups, channels // groups, extended.shape[2])
    summed = jnp.zeros((3, groups, channels // groups, length), jnp.float32)
    for offset in range(short_taps.shape[2]):
        window = shaped[:, :, :, reach_back - offset : reach_back - offset + length].astype(
            jnp.float32
        )
        summed = summed + short_taps[:, :, offset][:, :, None, None] * window
    return summed


def kernel_table(pole_rates, residues, block):
    row_index = jnp.arange(block, dtype=jnp.int32)[:, None]
    col_index = jnp.arange(block, dtype=jnp.int32)[None, :]
    lag_flat = (row_index - col_index).reshape(-1)
    step_values = jnp.arange(block, dtype=jnp.int32).astype(jnp.float32)
    modal_row = jnp.einsum(
        "gp,gpl->gl",
        residues,
        jnp.exp(-pole_rates[:, :, None] * step_values),
        precision=HIGHEST_PRECISION,
    )
    picker = (jnp.arange(block, dtype=jnp.int32)[:, None] == lag_flat[None, :]).astype(jnp.float32)
    table = jnp.dot(
        modal_row, picker, precision=HIGHEST_PRECISION, preferred_element_type=jnp.float32
    )
    return table.reshape(modal_row.shape[0], block, block)


def compose(earlier, later_pair):
    return (earlier[0] * later_pair[0], later_pair[0] * earlier[1] + later_pair[1])


def block_terms(product, kernel, pole_rates, block):
    groups, group_width, length = product.shape
    block_count = length // block
    current = product.reshape(groups, group_width, block_count, block)
    inner_part = jnp.einsum("gsnk,gik->gsni", current, kernel, precision=HIGHEST_PRECISION)
    reverse_steps = (block - 1 - jnp.arange(block, dtype=jnp.int32)).astype(jnp.float32)
    backward = jnp.exp(-pole_rates[:, :, None] * reverse_steps)
    end_states = jnp.einsum("gsnk,gpk->gsnp", current, backward, precision=HIGHEST_PRECISION)
    decays = jnp.broadcast_to(jnp.exp(-pole_rates * block)[:, None, None, :], end_states.shape)
    lifted, prefix = lax.associative_scan(compose, (decays, end_states), axis=2)
    return (inner_part, prefix)


def finish_terms(inner_part, prefix, state_in, pole_rates, residues, block):
    groups, group_width, block_count, block_size = inner_part.shape
    counts = jnp.arange(1, block_count + 1, dtype=jnp.int32).astype(jnp.float32) * block
    powers = jnp.exp(-pole_rates[:, None, :] * counts[None, :, None])
    after_block = prefix + powers[:, None, :, :] * state_in[:, :, None, :]
    starts = jnp.concatenate([state_in[:, :, None, :], after_block[:, :, :-1, :]], axis=2)
    lift_steps = jnp.arange(1, block + 1, dtype=jnp.int32).astype(jnp.float32)
    lift_table = residues[:, :, None] * jnp.exp(-pole_rates[:, :, None] * lift_steps)
    carried = jnp.einsum("gsnp,gpi->gsni", starts, lift_table, precision=HIGHEST_PRECISION)
    return (inner_part + carried).reshape(groups, group_width, block_count * block)


def shards(streams, short_taps, pole_rates, residues, skip, gain):
    relaid = lax.all_to_all(streams, "ctx", split_axis=2, concat_axis=1, tiled=True)
    channels = relaid.shape[1]
    length = relaid.shape[2]
    groups = pole_rates.shape[0]
    group_width = channels // groups
    left_edge = passed_along(relaid[:, :, length - (SHORT - 1) :], "ctx", 1)
    filtered = short_filter(
        jnp.concatenate([left_edge, relaid], axis=2), short_taps, groups, length
    )
    product = filtered[1] * filtered[2]
    kernel = kernel_table(pole_rates, residues, BLOCK)
    inner_part, prefix = block_terms(product, kernel, pole_rates, BLOCK)
    own_state = prefix[:, :, -1, :]
    device_decay = jnp.broadcast_to(jnp.exp(-pole_rates * length)[:, None, :], own_state.shape)

    def advance(step_index, incoming):
        return passed_along(device_decay * incoming + own_state, "ctx", 1)

    state_in = lax.fori_loop(0, lax.axis_size("ctx") - 1, advance, jnp.zeros_like(own_state))
    convolved = finish_terms(inner_part, prefix, state_in, pole_rates, residues, BLOCK)
    gated_value = filtered[0] * (
        convolved + skip.reshape(groups, group_width)[:, :, None] * product
    )
    partial_sum = jnp.sum(gated_value * gated_value, axis=(0, 1))
    mean_square = lax.psum(partial_sum, "ch") / D
    scaled = (
        gated_value.reshape(channels, length)
        * gain[:, None]
        * lax.rsqrt(mean_square + 1e-05)[None, :]
    )
    return scaled.astype(jnp.bfloat16)


def solution(mesh):
    placed = (
        P(None, ("ch", "ctx"), None),
        P(None, "ch", None),
        P("ch", None),
        P("ch", None),
        P("ch"),
        P("ch"),
    )
    return jax.shard_map(
        shards, mesh=mesh, in_specs=placed, out_specs=P("ch", "ctx"), check_vma=False
    )
```

profile of v0, /device:TPU:10, one launch (start us, length us, event | category | flops | bytes accessed | tf_op | source)
XLA Modules:
  0.0 251.8 jit_solution(15154524518168503117)
XLA Ops:
  0.0 7.2 %copy.81 = bf16[3,256,2048]{1,0,2:T(4,128)(2,1)} copy(bf16[3,256,2048]{2,1,0:T(8,128)(2,1)} %param.8) | data formatting | bytes 6291456 | tf_op args[0]
  7.2 6.4 %all-to-all-start = ((bf16[3,256,2048]{1,0,2:T(4,128)(2,1)}), bf16[3,256,2048]{1,0,2:T(4,128)(2,1)}, u32[]{:S(2)}, u32[]{:S(2)}) async-start(bf16[3,256,2048]{1,0,2:T(4,128)(2,1)} %copy.81), calls=%async_computation | async-start | bytes 8388608 | tf_op jit(solution)/shard_map/all_to_all | solution.py:81
  15.1 4.4 %fusion.6 = f32[16,8,128,128]{3,1,2,0:T(8,128)S(1)} fusion(f32[128,128]{1,0:T(8,128)S(1)} %bitcast.92, s32[16384]{0:T(1024)S(1)} %subtract_bitcast_fusion), kind=kOutput, calls=%fused_computation.18 | convolution fusion | flops 3223322624 | bytes 8519680 | tf_op jit(solution)/shard_map/dot_general | solution.py:45
  19.6 4.7 %copy.112 = f32[16,8,128,128]{3,2,1,0:T(8,128)} copy(f32[16,8,128,128]{3,1,2,0:T(8,128)S(1)} %fusion.6) | data formatting | bytes 16777216
  25.3 78.2 %all-to-all-done = bf16[3,256,2048]{1,0,2:T(4,128)(2,1)} async-done(((bf16[3,256,2048]{1,0,2:T(4,128)(2,1)}), bf16[3,256,2048]{1,0,2:T(4,128)(2,1)}, u32[]{:S(2)}, u32[]{:S(2)}) %all-to-all-start) | async-done | bytes 3145760 | tf_op jit(solution)/shard_map/all_to_all | solution.py:81
  103.4 4.3 %copy.82 = bf16[3,256,2048]{1,2,0:T(8,128)(2,1)} copy(bf16[3,256,2048]{1,0,2:T(4,128)(2,1)} %all-to-all-done) | data formatting | bytes 6291456 | tf_op jit(solution)/shard_map/all_to_all | solution.py:81
  107.7 3.2 %copy.83 = bf16[3,8,256,256]{3,2,1,0:T(8,128)(2,1)S(1)} copy(bf16[3,8,256,256]{2,3,1,0:T(8,128)(2,1)} %bitcast.86) | data formatting | bytes 6291456 | tf_op jit(solution)/shard_map/all_to_all | solution.py:81
  114.4 3.6 %collective-permute-start.1 = (bf16[3,2048,6]{1,2,0:T(8,128)(2,1)S(1)}, bf16[3,2048,6]{1,2,0:T(8,128)(2,1)}, u32[]{:S(2)}, u32[]{:S(2)}) collective-permute-start(bf16[3,2048,6]{1,2,0:T(8,128)(2,1)S(1)} %copy.85), channel_id=1, source_target_pairs={{0,4},{4,8},{8,12},{12,16},{16,20},{20,24},{24,28},{1,5},{5,9},{9,... | collective-permute-start | bytes 221192 | tf_op jit(solution)/shard_map/ppermute | solution.py:17
  117.9 3.1 %collective-permute-done.1 = bf16[3,2048,6]{1,2,0:T(8,128)(2,1)} collective-permute-done((bf16[3,2048,6]{1,2,0:T(8,128)(2,1)S(1)}, bf16[3,2048,6]{1,2,0:T(8,128)(2,1)}, u32[]{:S(2)}, u32[]{:S(2)}) %collective-permute-start.1) | collective-permute-done | bytes 73760 | tf_op jit(solution)/shard_map/ppermute | solution.py:17
  123.5 15.2 %multiply_add_fusion.1 = f32[3,128,16,256]{3,2,1,0:T(8,128)S(1)} fusion(bf16[3,128,16,256]{3,2,1,0:T(8,128)(2,1)S(1)} %bitcast.85, bf16[3,128,16,6]{3,2,1,0:T(8,128)(2,1)} %bitcast.91, f32[3,128]{1,0:T(4,128)S(1)} %get-tuple-element.85, f32[3,128]{1,0:T(4,128)S(1)} %get-tuple-element.86, f32[3,128]{1,0:T(4,128)S(1)} %get-tuple-element.87, ...), kind=kLoop, calls=%fused_computation.11 | loop fusion | flops 59768832 | bytes 9521664 | tf_op jit(solution)/shard_map/add | solution.py:29
  143.9 3.0 %copy.89 = f32[128,16,2,128]{3,1,2,0:T(8,128)} copy(f32[128,16,2,128]{0,3,2,1:T(8,128)} %bitcast.89) | data formatting | bytes 4194304 | tf_op jit(solution)/shard_map/mul | solution.py:90
  146.9 16.8 %fusion.2 = f32[128,16,2,128]{3,1,2,0:T(8,128)} fusion(f32[128,16,2,128]{3,1,2,0:T(8,128)} %copy.89, f32[128,128,128,1]{2,1,0,3:T(8,128)} %bitcast.83), kind=kOutput, calls=%fused_computation.7 | convolution fusion | flops 805306368 | bytes 12582912 | tf_op jit(solution)/shard_map/gsnk,gik->gsni/dot_general | solution.py:59
  167.9 56.0 %while.11 = (s32[]{:T(128)}, f32[128,16,16]{0,2,1:T(8,128)S(1)}, f32[128,16,16]{0,2,1:T(8,128)S(1)}, f32[128,16]{0,1:T(8,128)S(1)}, s32[]{:T(128)}) while((s32[]{:T(128)}, f32[128,16,16]{0,2,1:T(8,128)S(1)}, f32[128,16,16]{0,2,1:T(8,128)S(1)}, f32[128,16]{0,1:T(8,128)S(1)}, s32[]{:T(128)}) %tuple.40), condition=%wide.region_1.0_spmd.clone, body=%wide.region_0.0_spmd.clone.sunk | while | flops 65538 | bytes 925797 | solution.py:99
  167.9 4.2 %collective-permute-start = (f32[128,16,16]{0,2,1:T(8,128)S(1)}, f32[128,16,16]{0,2,1:T(8,128)S(1)}, u32[]{:S(2)}, u32[]{:S(2)}) collective-permute-start(f32[128,16,16]{0,2,1:T(8,128)S(1)} %multiply_add_fusion.3), channel_id=1, source_target_pairs={{0,4},{4,8},{8,12},{12,16},{16,20},{20,24},{24,28},{1,5},{5,9},{9,... | collective-permute-start | bytes 393224 | tf_op jit(solution)/shard_map/while/body/eval_jaxpr/ppermute | solution.py:17
  172.1 3.4 %collective-permute-done = f32[128,16,16]{0,2,1:T(8,128)S(1)} collective-permute-done((f32[128,16,16]{0,2,1:T(8,128)S(1)}, f32[128,16,16]{0,2,1:T(8,128)S(1)}, u32[]{:S(2)}, u32[]{:S(2)}) %collective-permute-start) | collective-permute-done | bytes 131104 | tf_op jit(solution)/shard_map/while/body/eval_jaxpr/ppermute | solution.py:17
  175.5 4.4 %collective-permute-start = (f32[128,16,16]{0,2,1:T(8,128)S(1)}, f32[128,16,16]{0,2,1:T(8,128)S(1)}, u32[]{:S(2)}, u32[]{:S(2)}) collective-permute-start(f32[128,16,16]{0,2,1:T(8,128)S(1)} %multiply_add_fusion.3), channel_id=1, source_target_pairs={{0,4},{4,8},{8,12},{12,16},{16,20},{20,24},{24,28},{1,5},{5,9},{9,... | collective-permute-start | bytes 393224 | tf_op jit(solution)/shard_map/while/body/eval_jaxpr/ppermute | solution.py:17
  179.9 3.4 %collective-permute-done = f32[128,16,16]{0,2,1:T(8,128)S(1)} collective-permute-done((f32[128,16,16]{0,2,1:T(8,128)S(1)}, f32[128,16,16]{0,2,1:T(8,128)S(1)}, u32[]{:S(2)}, u32[]{:S(2)}) %collective-permute-start) | collective-permute-done | bytes 131104 | tf_op jit(solution)/shard_map/while/body/eval_jaxpr/ppermute | solution.py:17
  183.3 4.4 %collective-permute-start = (f32[128,16,16]{0,2,1:T(8,128)S(1)}, f32[128,16,16]{0,2,1:T(8,128)S(1)}, u32[]{:S(2)}, u32[]{:S(2)}) collective-permute-start(f32[128,16,16]{0,2,1:T(8,128)S(1)} %multiply_add_fusion.3), channel_id=1, source_target_pairs={{0,4},{4,8},{8,12},{12,16},{16,20},{20,24},{24,28},{1,5},{5,9},{9,... | collective-permute-start | bytes 393224 | tf_op jit(solution)/shard_map/while/body/eval_jaxpr/ppermute | solution.py:17
  187.7 3.4 %collective-permute-done = f32[128,16,16]{0,2,1:T(8,128)S(1)} collective-permute-done((f32[128,16,16]{0,2,1:T(8,128)S(1)}, f32[128,16,16]{0,2,1:T(8,128)S(1)}, u32[]{:S(2)}, u32[]{:S(2)}) %collective-permute-start) | collective-permute-done | bytes 131104 | tf_op jit(solution)/shard_map/while/body/eval_jaxpr/ppermute | solution.py:17
  191.1 4.4 %collective-permute-start = (f32[128,16,16]{0,2,1:T(8,128)S(1)}, f32[128,16,16]{0,2,1:T(8,128)S(1)}, u32[]{:S(2)}, u32[]{:S(2)}) collective-permute-start(f32[128,16,16]{0,2,1:T(8,128)S(1)} %multiply_add_fusion.3), channel_id=1, source_target_pairs={{0,4},{4,8},{8,12},{12,16},{16,20},{20,24},{24,28},{1,5},{5,9},{9,... | collective-permute-start | bytes 393224 | tf_op jit(solution)/shard_map/while/body/eval_jaxpr/ppermute | solution.py:17
  195.5 3.9 %collective-permute-done = f32[128,16,16]{0,2,1:T(8,128)S(1)} collective-permute-done((f32[128,16,16]{0,2,1:T(8,128)S(1)}, f32[128,16,16]{0,2,1:T(8,128)S(1)}, u32[]{:S(2)}, u32[]{:S(2)}) %collective-permute-start) | collective-permute-done | bytes 131104 | tf_op jit(solution)/shard_map/while/body/eval_jaxpr/ppermute | solution.py:17
  199.5 5.0 %collective-permute-start = (f32[128,16,16]{0,2,1:T(8,128)S(1)}, f32[128,16,16]{0,2,1:T(8,128)S(1)}, u32[]{:S(2)}, u32[]{:S(2)}) collective-permute-start(f32[128,16,16]{0,2,1:T(8,128)S(1)} %multiply_add_fusion.3), channel_id=1, source_target_pairs={{0,4},{4,8},{8,12},{12,16},{16,20},{20,24},{24,28},{1,5},{5,9},{9,... | collective-permute-start | bytes 393224 | tf_op jit(solution)/shard_map/while/body/eval_jaxpr/ppermute | solution.py:17
  204.5 4.0 %collective-permute-done = f32[128,16,16]{0,2,1:T(8,128)S(1)} collective-permute-done((f32[128,16,16]{0,2,1:T(8,128)S(1)}, f32[128,16,16]{0,2,1:T(8,128)S(1)}, u32[]{:S(2)}, u32[]{:S(2)}) %collective-permute-start) | collective-permute-done | bytes 131104 | tf_op jit(solution)/shard_map/while/body/eval_jaxpr/ppermute | solution.py:17
  208.6 4.3 %collective-permute-start = (f32[128,16,16]{0,2,1:T(8,128)S(1)}, f32[128,16,16]{0,2,1:T(8,128)S(1)}, u32[]{:S(2)}, u32[]{:S(2)}) collective-permute-start(f32[128,16,16]{0,2,1:T(8,128)S(1)} %multiply_add_fusion.3), channel_id=1, source_target_pairs={{0,4},{4,8},{8,12},{12,16},{16,20},{20,24},{24,28},{1,5},{5,9},{9,... | collective-permute-start | bytes 393224 | tf_op jit(solution)/shard_map/while/body/eval_jaxpr/ppermute | solution.py:17
  212.8 3.4 %collective-permute-done = f32[128,16,16]{0,2,1:T(8,128)S(1)} collective-permute-done((f32[128,16,16]{0,2,1:T(8,128)S(1)}, f32[128,16,16]{0,2,1:T(8,128)S(1)}, u32[]{:S(2)}, u32[]{:S(2)}) %collective-permute-start) | collective-permute-done | bytes 131104 | tf_op jit(solution)/shard_map/while/body/eval_jaxpr/ppermute | solution.py:17
  216.3 4.4 %collective-permute-start = (f32[128,16,16]{0,2,1:T(8,128)S(1)}, f32[128,16,16]{0,2,1:T(8,128)S(1)}, u32[]{:S(2)}, u32[]{:S(2)}) collective-permute-start(f32[128,16,16]{0,2,1:T(8,128)S(1)} %multiply_add_fusion.3), channel_id=1, source_target_pairs={{0,4},{4,8},{8,12},{12,16},{16,20},{20,24},{24,28},{1,5},{5,9},{9,... | collective-permute-start | bytes 393224 | tf_op jit(solution)/shard_map/while/body/eval_jaxpr/ppermute | solution.py:17
  220.6 3.2 %collective-permute-done = f32[128,16,16]{0,2,1:T(8,128)S(1)} collective-permute-done((f32[128,16,16]{0,2,1:T(8,128)S(1)}, f32[128,16,16]{0,2,1:T(8,128)S(1)}, u32[]{:S(2)}, u32[]{:S(2)}) %collective-permute-start) | collective-permute-done | bytes 131104 | tf_op jit(solution)/shard_map/while/body/eval_jaxpr/ppermute | solution.py:17
  226.2 3.7 %fusion.24 = f32[128,16,2,128]{3,1,2,0:T(8,128)} fusion(f32[128,16,2,128]{3,1,2,0:T(8,128)S(1)} %copy-done.4, f32[128,16,1,16]{3,1,2,0:T(8,128)S(1)} %fusion.29, f32[128,16,1,16]{3,1,2,0:T(8,128)S(1)} %bitcast.87, f32[128]{0:T(128)S(1)} %add_convert_fusion, f32[128,16]{1,0:T(8,128)S(1)} %copy.96, f32[128,16]{1,0:T(8,128)S(1)} %copy.88), kind=kOutput, calls=%fused_computation.43 | convolution fusion | flops 101777408 | bytes 4473344 | tf_op jit(solution)/shard_map/gsnp,gpi->gsni/dot_general | solution.py:76
  229.9 4.0 %copy.97 = f32[128,16,2,128]{3,2,1,0:T(2,128)} copy(f32[128,16,2,128]{3,1,2,0:T(8,128)} %fusion.24) | data formatting | bytes 4194304 | tf_op jit(solution)/shard_map/add | solution.py:77
  236.9 3.1 %copy.99 = f32[128,16,256]{2,1,0:T(8,128)} copy(f32[128,16,256]{0,2,1:T(8,128)} %bitcast.88) | data formatting | bytes 4194304 | tf_op jit(solution)/shard_map/reshape | solution.py:77
  242.7 5.7 %psum.7 = f32[256]{0:T(256)S(1)} all-reduce(f32[256]{0:T(256)S(1)} %fusion.23), channel_id=1, replica_groups=mesh['ctx'=8,'ch'=4] {'ch'}, use_global_device_ids=true, to_apply=%region_3.0 | all-reduce | flops 256 | bytes 2048 | tf_op jit(solution)/shard_map/psum | solution.py:105
  248.4 3.4 %fusion.15 = bf16[2048,256]{1,0:T(8,128)(2,1)} fusion(f32[256,8,2,128]{3,2,1,0:T(2,128)} %bitcast.90, f32[1,128,16,256]{3,2,1,0:T(8,128)S(1)} %get-tuple-element.72, f32[1,128,16,256]{3,2,1,0:T(8,128)} %get-tuple-element.71, f32[256]{0:T(256)S(1)} %add_rsqrt_fusion, f32[2048]{0:T(1024)S(1)} %copy-done.11, f32[2048]{0:T(1024)S(1)} %copy-done.8), kind=kLoop, calls=%fused_computation.29 | loop fusion | flops 3145728 | bytes 7357440 | tf_op jit(solution)/shard_map/convert_element_type | solution.py:111
  (66 shorter events, 25.9 us)
Async XLA Ops:
  7.2 6.4 %copy-start.9 = (f32[3,128,7]{1,2,0:T(8,128)S(1)}, f32[3,128,7]{1,2,0:T(8,128)}, u32[]{:S(2)}) copy-start(f32[3,128,7]{1,2,0:T(8,128)} %param.9) | copy-start | bytes 32260
  7.2 6.4 %copy-start.7 = (f32[128,16]{0,1:T(8,128)S(1)}, f32[128,16]{0,1:T(8,128)}, u32[]{:S(2)}) copy-start(f32[128,16]{0,1:T(8,128)} %param.11) | copy-start | bytes 24580
  7.2 6.6 %copy-start.10 = (f32[128,16]{0,1:T(8,128)S(1)}, f32[128,16]{0,1:T(8,128)}, u32[]{:S(2)}) copy-start(f32[128,16]{0,1:T(8,128)} %param.10) | copy-start | bytes 24580
  7.2 96.3 %all-to-all-start = ((bf16[3,256,2048]{1,0,2:T(4,128)(2,1)}), bf16[3,256,2048]{1,0,2:T(4,128)(2,1)}, u32[]{:S(2)}, u32[]{:S(2)}) async-start(bf16[3,256,2048]{1,0,2:T(4,128)(2,1)} %copy.81), calls=%async_computation | async-start | bytes 8388608 | tf_op jit(solution)/shard_map/all_to_all | solution.py:81
  19.5 5.0 %copy-start.8 = (f32[2048]{0:T(1024)S(1)}, f32[2048]{0:T(1024)}, u32[]{:S(2)}) copy-start(f32[2048]{0:T(1024)} %param.12) | copy-start | bytes 24580
  24.5 83.2 %copy-start.5 = (f32[128,2,16]{2,1,0:T(2,128)}, f32[128,2,16]{2,1,0:T(2,128)S(1)}, u32[]{:S(2)}) copy-start(f32[128,2,16]{2,1,0:T(2,128)S(1)} %multiply_exponential_fusion) | copy-start | bytes 49156
  114.4 6.7 %collective-permute-start.1 = (bf16[3,2048,6]{1,2,0:T(8,128)(2,1)S(1)}, bf16[3,2048,6]{1,2,0:T(8,128)(2,1)}, u32[]{:S(2)}, u32[]{:S(2)}) collective-permute-start(bf16[3,2048,6]{1,2,0:T(8,128)(2,1)S(1)} %copy.85), channel_id=1, source_target_pairs={{0,4},{4,8},{8,12},{12,16},{16,20},{20,24},{24,28},{1,5},{5,9},{9,... | collective-permute-start | bytes 221192 | tf_op jit(solution)/shard_map/ppermute | solution.py:17
  138.7 3.3 %copy-start = (f32[3,128,16,256]{3,2,1,0:T(8,128)}, f32[3,128,16,256]{3,2,1,0:T(8,128)S(1)}, u32[]{:S(2)}) copy-start(f32[3,128,16,256]{3,2,1,0:T(8,128)S(1)} %multiply_add_fusion.1) | copy-start | bytes 18874372
  146.9 16.8 %copy-start.1 = (f32[128,16,2,128]{3,1,2,0:T(8,128)S(1)}, f32[128,16,2,128]{3,1,2,0:T(8,128)}, u32[]{:S(2)}) copy-start(f32[128,16,2,128]{3,1,2,0:T(8,128)} %copy.89) | copy-start | bytes 6291460
  166.1 1.0 copy-start.2
  166.1 1.3 copy-start.3
  167.4 57.0 %slice-start = ((f32[128,2,16]{2,1,0:T(2,128)}), f32[128,1,16]{2,1,0:T(1,128)S(1)}, s32[]{:S(2)}) async-start(f32[128,2,16]{2,1,0:T(2,128)} %copy-done.5), calls=%async_computation.1 | async-start | bytes 131072 | tf_op jit(solution)/shard_map/slice | solution.py:73
  167.9 7.6 %collective-permute-start = (f32[128,16,16]{0,2,1:T(8,128)S(1)}, f32[128,16,16]{0,2,1:T(8,128)S(1)}, u32[]{:S(2)}, u32[]{:S(2)}) collective-permute-start(f32[128,16,16]{0,2,1:T(8,128)S(1)} %multiply_add_fusion.3), channel_id=1, source_target_pairs={{0,4},{4,8},{8,12},{12,16},{16,20},{20,24},{24,28},{1,5},{5,9},{9,... | collective-permute-start | bytes 393224 | tf_op jit(solution)/shard_map/while/body/eval_jaxpr/ppermute | solution.py:17
  175.5 7.8 %collective-permute-start = (f32[128,16,16]{0,2,1:T(8,128)S(1)}, f32[128,16,16]{0,2,1:T(8,128)S(1)}, u32[]{:S(2)}, u32[]{:S(2)}) collective-permute-start(f32[128,16,16]{0,2,1:T(8,128)S(1)} %multiply_add_fusion.3), channel_id=1, source_target_pairs={{0,4},{4,8},{8,12},{12,16},{16,20},{20,24},{24,28},{1,5},{5,9},{9,... | collective-permute-start | bytes 393224 | tf_op jit(solution)/shard_map/while/body/eval_jaxpr/ppermute | solution.py:17
  183.3 7.8 %collective-permute-start = (f32[128,16,16]{0,2,1:T(8,128)S(1)}, f32[128,16,16]{0,2,1:T(8,128)S(1)}, u32[]{:S(2)}, u32[]{:S(2)}) collective-permute-start(f32[128,16,16]{0,2,1:T(8,128)S(1)} %multiply_add_fusion.3), channel_id=1, source_target_pairs={{0,4},{4,8},{8,12},{12,16},{16,20},{20,24},{24,28},{1,5},{5,9},{9,... | collective-permute-start | bytes 393224 | tf_op jit(solution)/shard_map/while/body/eval_jaxpr/ppermute | solution.py:17
  191.1 8.4 %collective-permute-start = (f32[128,16,16]{0,2,1:T(8,128)S(1)}, f32[128,16,16]{0,2,1:T(8,128)S(1)}, u32[]{:S(2)}, u32[]{:S(2)}) collective-permute-start(f32[128,16,16]{0,2,1:T(8,128)S(1)} %multiply_add_fusion.3), channel_id=1, source_target_pairs={{0,4},{4,8},{8,12},{12,16},{16,20},{20,24},{24,28},{1,5},{5,9},{9,... | collective-permute-start | bytes 393224 | tf_op jit(solution)/shard_map/while/body/eval_jaxpr/ppermute | solution.py:17
  199.5 9.1 %collective-permute-start = (f32[128,16,16]{0,2,1:T(8,128)S(1)}, f32[128,16,16]{0,2,1:T(8,128)S(1)}, u32[]{:S(2)}, u32[]{:S(2)}) collective-permute-start(f32[128,16,16]{0,2,1:T(8,128)S(1)} %multiply_add_fusion.3), channel_id=1, source_target_pairs={{0,4},{4,8},{8,12},{12,16},{16,20},{20,24},{24,28},{1,5},{5,9},{9,... | collective-permute-start | bytes 393224 | tf_op jit(solution)/shard_map/while/body/eval_jaxpr/ppermute | solution.py:17
  208.6 7.7 %collective-permute-start = (f32[128,16,16]{0,2,1:T(8,128)S(1)}, f32[128,16,16]{0,2,1:T(8,128)S(1)}, u32[]{:S(2)}, u32[]{:S(2)}) collective-permute-start(f32[128,16,16]{0,2,1:T(8,128)S(1)} %multiply_add_fusion.3), channel_id=1, source_target_pairs={{0,4},{4,8},{8,12},{12,16},{16,20},{20,24},{24,28},{1,5},{5,9},{9,... | collective-permute-start | bytes 393224 | tf_op jit(solution)/shard_map/while/body/eval_jaxpr/ppermute | solution.py:17
  216.3 7.6 %collective-permute-start = (f32[128,16,16]{0,2,1:T(8,128)S(1)}, f32[128,16,16]{0,2,1:T(8,128)S(1)}, u32[]{:S(2)}, u32[]{:S(2)}) collective-permute-start(f32[128,16,16]{0,2,1:T(8,128)S(1)} %multiply_add_fusion.3), channel_id=1, source_target_pairs={{0,4},{4,8},{8,12},{12,16},{16,20},{20,24},{24,28},{1,5},{5,9},{9,... | collective-permute-start | bytes 393224 | tf_op jit(solution)/shard_map/while/body/eval_jaxpr/ppermute | solution.py:17
  224.3 1.9 copy-start.4
  236.9 3.1 %copy-start.6 = (f32[128,16]{1,0:T(8,128)S(1)}, f32[128,16]{1,0:T(8,128)}, u32[]{:S(2)}) copy-start(f32[128,16]{1,0:T(8,128)} %mul.272) | copy-start | bytes 24580
  240.0 8.4 %copy-start.11 = (f32[2048]{0:T(1024)S(1)}, f32[2048]{0:T(1024)}, u32[]{:S(2)}) copy-start(f32[2048]{0:T(1024)} %param.13) | copy-start | bytes 24580
where the time goes:
time: 256 us; the launch traced here: 252 us
  waiting for transfers between devices  106 us (41%)
  local copies, waits for them, and re-layouts  44.7 us (17%)
  starting transfers between devices  40.9 us (16%)
  matrix products  28.2 us (11%)
  other arithmetic  26 us (10%)
  blocking collectives  5.66 us (2%)
    all_to_all x1, waiting for transfers between devices, shards(): lax.all_to_all(streams, 'ctx', split_axis=2, concat_axis=1, tiled=True)  78.2 us
    ppermute x8, starting transfers between devices, passed_along(): return lax.ppermute(array, axis, pairs)  34.5 us
    ppermute x8, waiting for transfers between devices, passed_along(): return lax.ppermute(array, axis, pairs)  27.9 us
    dot_general x1, matrix products, block_terms(): jnp.einsum('gsnk,gik->gsni', current, kernel, precision=HIGHEST_PRECISION)  16.8 us
    add x1, other arithmetic, short_filter(): summed = summed + short_taps[:, :, offset][:, :, None, None] * window  15.2 us
    unnamed x33, local copies, waits for them, and re-layouts  14.9 us
    all_to_all x2, local copies, waits for them, and re-layouts, shards(): lax.all_to_all(streams, 'ctx', split_axis=2, concat_axis=1, tiled=True)  7.44 us
    add x2, local copies, waits for them, and re-layouts, finish_terms(): inner_part + carried  6.98 us
  transfers between devices with their start and end apart: 9, of which 9 were waited for; matrix products, arithmetic and copies ran while one was open for 5% of the time, Pallas kernels for 0%

commit v1 on v0

v1 whole, which is shorter than its diff:
```python
import functools

import jax
import jax.numpy as jnp
from jax import lax
from jax.experimental import pallas as pl
from jax.experimental.pallas import tpu as pltpu
from jax.sharding import PartitionSpec as P

BLOCK = 128


def split(value):
    high = value.astype(jnp.bfloat16)
    low = (value - high.astype(jnp.float32)).astype(jnp.bfloat16)
    return high, low


def halves(array):
    return array[:, :BLOCK] + array[:, BLOCK:]


def rolled(row):
    return pltpu.roll(
        jnp.broadcast_to(row, (BLOCK, BLOCK)), 0, 1, stride=1, stride_axis=0
    )


def mix(streams_ref, taps_ref, columns_ref, gated_ref, sums_ref, squares):
    step = pl.program_id(0)
    width, length = streams_ref.shape[1:]
    blocks = length // BLOCK
    per_device = gated_ref.shape[2] // BLOCK
    row_index = lax.broadcasted_iota(jnp.int32, (BLOCK, BLOCK), 0)
    col_index = lax.broadcasted_iota(jnp.int32, (BLOCK, BLOCK), 1)
    causal = col_index >= row_index

    filtered = []
    for m in range(3):
        table = rolled(taps_ref[0, m : m + 1, :])
        high_now, low_now = split(jnp.where(causal, table, 0.0))
        high_before, low_before = split(jnp.where(causal, 0.0, table))
        weights = jnp.concatenate(
            [
                jnp.concatenate([high_before, low_before], axis=1),
                jnp.concatenate([high_now, low_now], axis=1),
            ],
            axis=0,
        )
        pieces = [streams_ref[m, :, n * BLOCK : (n + 1) * BLOCK] for n in range(blocks)]
        now = jnp.concatenate(pieces, axis=0)
        before = jnp.concatenate([jnp.zeros_like(pieces[0])] + pieces[:-1], axis=0)
        both = jnp.concatenate([before, now], axis=1)
        filtered.append(halves(jnp.dot(both, weights, preferred_element_type=jnp.float32)))
    product = filtered[1] * filtered[2]
    product_high, product_low = split(product)
    pair = jnp.concatenate([product_high, product_low], axis=1)

    skip = columns_ref[:, 0:1]
    gain = columns_ref[:, 1:2]
    rates = columns_ref[:, 2:3]
    residues = columns_ref[:, 3:4]
    lags = lax.broadcasted_iota(jnp.int32, (width, BLOCK), 1).astype(jnp.float32)
    modes = residues * jnp.exp(-rates * lags)
    table_high, table_low = split(
        jnp.where(causal, rolled(jnp.sum(modes, axis=0, keepdims=True)), 0.0)
    )
    table_row = jnp.concatenate([table_high, table_low], axis=1)
    summed = jnp.dot(
        pair,
        jnp.concatenate([table_row, table_row], axis=0),
        preferred_element_type=jnp.float32,
    )

    back_high, back_low = split(jnp.exp(-rates * (BLOCK - 1 - lags)))
    back = jnp.concatenate(
        [
            jnp.concatenate([back_high, back_high], axis=1),
            jnp.concatenate([back_low, back_low], axis=1),
        ],
        axis=0,
    )
    ends = lax.dot_general(
        back, pair, (((1,), (1,)), ((), ())), preferred_element_type=jnp.float32
    )
    states = ends[:width] + ends[width:]
    lane = lax.broadcasted_iota(jnp.int32, states.shape, 1)
    reach = 1
    while reach < blocks:
        earlier = pltpu.roll(states, reach * width, 1)
        decay = jnp.exp(-rates * (BLOCK * reach))
        states = states + jnp.where(lane >= reach * width, decay * earlier, 0.0)
        reach *= 2
    starts = jnp.where(lane >= width, pltpu.roll(states, width, 1), 0.0)
    starts_high, starts_low = split(starts)
    starts = jnp.concatenate(
        [starts_high.astype(jnp.float32), starts_low.astype(jnp.float32)], axis=0
    ).T.astype(jnp.bfloat16)
    lift_high, lift_low = split(residues * jnp.exp(-rates * (lags + 1.0)))
    lift_row = jnp.concatenate([lift_high, lift_low], axis=1)
    summed = summed + jnp.dot(
        starts,
        jnp.concatenate([lift_row, lift_row], axis=0),
        preferred_element_type=jnp.float32,
    )

    shaped = (blocks, width, BLOCK)
    gated = filtered[0].reshape(shaped) * (
        halves(summed).reshape(shaped) + skip[None] * product.reshape(shaped)
    )
    squared = jnp.sum((gated * gated).reshape(blocks, width // 8, 8, BLOCK), axis=1)

    @pl.when(step == 0)
    def _():
        squares[...] = squared

    @pl.when(step > 0)
    def _():
        squares[...] += squared

    scaled = gated * gain[None]
    for n in range(blocks):
        at = (n % per_device) * BLOCK
        gated_ref[n // per_device, :, at : at + BLOCK] = scaled[n]

    @pl.when(step == pl.num_programs(0) - 1)
    def _():
        for n in range(blocks):
            at = (n % per_device) * BLOCK
            row = n // per_device
            sums_ref[row : row + 1, at : at + BLOCK] = jnp.sum(
                squares[n], axis=0, keepdims=True
            )


def shards(total_channels, streams, short_taps, pole_rates, residues, skip, gain):
    owners = lax.axis_size("ctx")
    me = lax.axis_index("ctx")
    channels, length = streams.shape[1:]
    groups = pole_rates.shape[0] // owners
    width = channels // groups
    assert pole_rates.shape[1] == width
    own = length // owners
    taps = lax.dynamic_slice_in_dim(short_taps, me * groups, groups, 1)
    taps = jnp.pad(taps.transpose(1, 0, 2), ((0, 0), (0, 0), (0, BLOCK - taps.shape[2])))
    columns = jnp.stack(
        [
            lax.dynamic_slice_in_dim(skip, me * channels, channels),
            lax.dynamic_slice_in_dim(gain, me * channels, channels),
            lax.dynamic_slice_in_dim(pole_rates, me * groups, groups).reshape(-1),
            lax.dynamic_slice_in_dim(residues, me * groups, groups).reshape(-1),
        ],
        axis=1,
    )
    gated, sums = pl.pallas_call(
        mix,
        grid=(groups,),
        in_specs=[
            pl.BlockSpec((3, width, length), lambda g: (0, g, 0)),
            pl.BlockSpec((1, 3, BLOCK), lambda g: (g, 0, 0)),
            pl.BlockSpec((width, 4), lambda g: (g, 0)),
        ],
        out_specs=[
            pl.BlockSpec((owners, width, own), lambda g: (0, g, 0)),
            pl.BlockSpec((owners, own), lambda g: (0, 0)),
        ],
        out_shape=[
            jax.ShapeDtypeStruct((owners, channels, own), jnp.float32),
            jax.ShapeDtypeStruct((owners, own), jnp.float32),
        ],
        scratch_shapes=[pltpu.VMEM((length // BLOCK, 8, BLOCK), jnp.float32)],
        compiler_params=pltpu.CompilerParams(vmem_limit_bytes=48 * 1024 * 1024),
    )(streams, taps, columns)
    mean_square = lax.psum(sums, ("ctx", "ch")) / total_channels
    scaled = (gated * lax.rsqrt(mean_square + 1e-05)[:, None, :]).astype(jnp.bfloat16)
    moved = lax.all_to_all(scaled, "ctx", split_axis=0, concat_axis=0, tiled=True)
    return moved.reshape(owners * channels, own)


def solution(mesh):
    placed = (
        P(None, ("ch", "ctx"), None),
        P(None, "ch", None),
        P("ch", None),
        P("ch", None),
        P("ch"),
        P("ch"),
    )

    def whole(streams, *others):
        return jax.shard_map(
            functools.partial(shards, streams.shape[1]),
            mesh=mesh,
            in_specs=placed,
            out_specs=P("ch", "ctx"),
            check_vma=False,
        )(streams, *others)

    return whole
```

time: 256 us -> 98.3 us (0.38)
  the two profiles are of different devices: /device:TPU:10 before, /device:TPU:0 now
where the time goes in v1:
time: 98.3 us; the launch traced here: 97.8 us
  blocking collectives  71.2 us (72%)
  Pallas kernels  20.5 us (21%)
  local copies, waits for them, and re-layouts  5.8 us (6%)
    psum x1, blocking collectives, shards(): mean_square = lax.psum(sums, ('ctx', 'ch')) / total_channels  42.1 us
    all_to_all x1, blocking collectives, shards(): lax.all_to_all(scaled, 'ctx', split_axis=0, concat_axis=0, tiled=True)  29.1 us
    pallas_call x1, Pallas kernels, shards(): pl.pallas_call(mix, grid=(groups,), in_specs=[pl.BlockSpec((3, width, len...  20.5 us
    unnamed x6, local copies, waits for them, and re-layouts  2.96 us

profile of v1, /device:TPU:0, one launch (start us, length us, event | category | flops | bytes accessed | tf_op | source)
XLA Modules:
  0.0 97.8 jit_solution(14813243535569274872)
XLA Ops:
  0.0 0.0 copy-start
  0.0 0.8 dynamic_slice.16
  0.8 0.8 dynamic_slice.17
  1.5 0.0 copy-done
  1.5 0.1 constant_dynamic-slice_fusion.2
  1.6 0.8 constant_dynamic-slice_fusion
  2.4 0.1 copy.19
  2.5 0.1 stack_reshape.7
  2.6 0.1 copy.18
  2.6 0.1 stack_reshape.6
  2.7 0.1 copy.21
  2.8 0.1 copy.20.columns_ref
  3.0 0.0 copy-start.1
  3.0 1.9 %copy-done.1 = bf16[3,256,2048]{2,1,0:T(8,128)(2,1)S(1)} copy-done((bf16[3,256,2048]{2,1,0:T(8,128)(2,1)S(1)}, bf16[3,256,2048]{2,1,0:T(8,128)(2,1)}, u32[]{:S(2)}) %copy-start.1) | copy-done | bytes 3145752
  4.9 20.5 %shard_map.64 = (f32[8,256,256]{2,1,0:T(8,128)S(1)}, f32[8,256]{1,0:T(8,128)S(1)}) custom-call(bf16[3,256,2048]{2,1,0:T(8,128)(2,1)S(1)} %copy-done.1, f32[16,3,128]{2,1,0:T(4,128)S(1)} %pad.4.taps_ref, f32[256,4]{1,0:T(8,128)S(1)} %copy.20.columns_ref), custom_call_target="tpu_custom_call" | custom-call | tf_op jit(solution)/shard_map/pallas_call | solution.py:155
  25.4 42.1 %psum.7 = f32[8,256]{1,0:T(8,128)S(1)} all-reduce(f32[8,256]{1,0:T(8,128)S(1)} %get-tuple-element.8), channel_id=1, replica_groups=mesh['ctx'=8,'ch'=4] {'ctx','ch'}, use_global_device_ids=true, to_apply=%region_0.1 | all-reduce | flops 2048 | bytes 16384 | tf_op jit(solution)/shard_map/psum | solution.py:174
  67.5 0.2 multiply_convert_fusion
  67.7 29.1 %all_to_all.5 = bf16[8,256,256]{2,1,0:T(8,128)(2,1)S(1)} all-to-all(bf16[8,256,256]{2,1,0:T(8,128)(2,1)S(1)} %multiply_convert_fusion), channel_id=1, replica_groups=mesh['ctx'=8,'ch'=4] {'ctx'}, dimensions={0} | all-to-all | bytes 2097152 | tf_op jit(solution)/shard_map/all_to_all | solution.py:176
  96.8 1.0 copy.23
  (3 shorter events, 0.0 us)
Async XLA Ops:
  0.0 1.5 %copy-start = (f32[3,128,7]{1,2,0:T(8,128)S(1)}, f32[3,128,7]{1,2,0:T(8,128)}, u32[]{:S(2)}) copy-start(f32[3,128,7]{1,2,0:T(8,128)} %param.7) | copy-start | bytes 32260
  3.0 1.9 %copy-start.1 = (bf16[3,256,2048]{2,1,0:T(8,128)(2,1)S(1)}, bf16[3,256,2048]{2,1,0:T(8,128)(2,1)}, u32[]{:S(2)}) copy-start(bf16[3,256,2048]{2,1,0:T(8,128)(2,1)} %streams_ref.1) | copy-start | bytes 9437188

commit v2 on v1

--- a/solution.py
+++ b/solution.py
@@ -8,6 +8,7 @@
 from jax.sharding import PartitionSpec as P
 
 BLOCK = 128
+MESH = pl.DeviceIdType.MESH
 
 
 def split(value):
@@ -26,18 +27,18 @@
     )
 
 
-def mix(streams_ref, taps_ref, columns_ref, gated_ref, sums_ref, squares):
-    step = pl.program_id(0)
-    width, length = streams_ref.shape[1:]
+def one_group(streams_ref, taps_ref, columns_ref, gated_ref, at_group, width):
+    length = streams_ref.shape[2]
     blocks = length // BLOCK
     per_device = gated_ref.shape[2] // BLOCK
+    rows = slice(at_group * width, (at_group + 1) * width)
     row_index = lax.broadcasted_iota(jnp.int32, (BLOCK, BLOCK), 0)
     col_index = lax.broadcasted_iota(jnp.int32, (BLOCK, BLOCK), 1)
     causal = col_index >= row_index
 
     filtered = []
     for m in range(3):
-        table = rolled(taps_ref[0, m : m + 1, :])
+        table = rolled(taps_ref[at_group, m : m + 1, :])
         high_now, low_now = split(jnp.where(causal, table, 0.0))
         high_before, low_before = split(jnp.where(causal, 0.0, table))
         weights = jnp.concatenate(
@@ -47,7 +48,7 @@
             ],
             axis=0,
         )
-        pieces = [streams_ref[m, :, n * BLOCK : (n + 1) * BLOCK] for n in range(blocks)]
+        pieces = [streams_ref[m, rows, n * BLOCK : (n + 1) * BLOCK] for n in range(blocks)]
         now = jnp.concatenate(pieces, axis=0)
         before = jnp.concatenate([jnp.zeros_like(pieces[0])] + pieces[:-1], axis=0)
         both = jnp.concatenate([before, now], axis=1)
@@ -56,10 +57,10 @@
     product_high, product_low = split(product)
     pair = jnp.concatenate([product_high, product_low], axis=1)
 
-    skip = columns_ref[:, 0:1]
-    gain = columns_ref[:, 1:2]
-    rates = columns_ref[:, 2:3]
-    residues = columns_ref[:, 3:4]
+    skip = columns_ref[rows, 0:1]
+    gain = columns_ref[rows, 1:2]
+    rates = columns_ref[rows, 2:3]
+    residues = columns_ref[rows, 3:4]
     lags = lax.broadcasted_iota(jnp.int32, (width, BLOCK), 1).astype(jnp.float32)
     modes = residues * jnp.exp(-rates * lags)
     table_high, table_low = split(
@@ -110,6 +111,24 @@
     )
     squared = jnp.sum((gated * gated).reshape(blocks, width // 8, 8, BLOCK), axis=1)
 
+    scaled = gated * gain[None]
+    for n in range(blocks):
+        at = (n % per_device) * BLOCK
+        gated_ref[n // per_device, rows, at : at + BLOCK] = scaled[n]
+
+    return squared
+
+
+def mix(at_once, streams_ref, taps_ref, columns_ref, gated_ref, sums_ref, squares):
+    step = pl.program_id(0)
+    width = streams_ref.shape[1] // at_once
+    blocks = streams_ref.shape[2] // BLOCK
+    per_device = gated_ref.shape[2] // BLOCK
+    parts = [
+        one_group(streams_ref, taps_ref, columns_ref, gated_ref, i, width) for i in range(at_once)
+    ]
+    squared = sum(parts[1:], parts[0])
+
     @pl.when(step == 0)
     def _():
         squares[...] = squared
@@ -117,11 +136,6 @@
     @pl.when(step > 0)
     def _():
         squares[...] += squared
-
-    scaled = gated * gain[None]
-    for n in range(blocks):
-        at = (n % per_device) * BLOCK
-        gated_ref[n // per_device, :, at : at + BLOCK] = scaled[n]
 
     @pl.when(step == pl.num_programs(0) - 1)
     def _():
@@ -131,6 +145,121 @@
             sums_ref[row : row + 1, at : at + BLOCK] = jnp.sum(
                 squares[n], axis=0, keepdims=True
             )
+
+
+def send(totals_of, sums_ref, gated_ref, out_ref, across, column, along, staged, scales, *sems):
+    across_sent, across_got, along_sent, along_got, block_sent, block_got, kept = sems
+    owners, channels, own = gated_ref.shape
+    across_count = lax.axis_size("ch")
+    me = lax.axis_index("ctx")
+    my_ch = lax.axis_index("ch")
+
+    def peer_ctx(by):
+        return {"ctx": lax.rem(me + by, owners)}
+
+    def peer_ch(by):
+        return {"ch": lax.rem(my_ch + by, across_count)}
+
+    barrier = pltpu.get_barrier_semaphore()
+
+    @pl.loop(1, across_count)
+    def _(by):
+        pl.semaphore_signal(barrier, inc=1, device_id=peer_ch(by), device_id_type=MESH)
+
+    @pl.loop(1, owners)
+    def _(by):
+        pl.semaphore_signal(barrier, inc=1, device_id=peer_ctx(by), device_id_type=MESH)
+
+    pl.semaphore_wait(barrier, across_count + owners - 2)
+
+    def across_copy(by):
+        return pltpu.make_async_remote_copy(
+            src_ref=sums_ref,
+            dst_ref=across.at[by],
+            send_sem=across_sent.at[by],
+            recv_sem=across_got.at[by],
+            device_id=peer_ch(by),
+            device_id_type=MESH,
+        )
+
+    def along_copy(by):
+        return pltpu.make_async_remote_copy(
+            src_ref=column,
+            dst_ref=along.at[by],
+            send_sem=along_sent.at[by],
+            recv_sem=along_got.at[by],
+            device_id=peer_ctx(by),
+            device_id_type=MESH,
+        )
+
+    def block_copy(by):
+        return pltpu.make_async_remote_copy(
+            src_ref=staged.at[by],
+            dst_ref=out_ref.at[pl.ds(pl.multiple_of(me * channels, 16), channels), :],
+            send_sem=block_sent.at[by],
+            recv_sem=block_got.at[by],
+            device_id=peer_ctx(by),
+            device_id_type=MESH,
+        )
+
+    def block_arrival(by):
+        source = lax.rem(me + owners - by, owners)
+        return pltpu.make_async_remote_copy(
+            src_ref=staged.at[by],
+            dst_ref=out_ref.at[pl.ds(pl.multiple_of(source * channels, 16), channels), :],
+            send_sem=block_sent.at[by],
+            recv_sem=block_got.at[by],
+            device_id=peer_ctx(by),
+            device_id_type=MESH,
+        )
+
+    @pl.loop(1, across_count)
+    def _(by):
+        across_copy(by).start()
+
+    column[...] = sums_ref[...]
+
+    @pl.loop(1, across_count)
+    def _(by):
+        across_copy(by).wait()
+        column[...] += across[by]
+
+    @pl.loop(1, owners)
+    def _(by):
+        along_copy(by).start()
+
+    scales[...] = column[...]
+
+    @pl.loop(1, owners)
+    def _(by):
+        along_copy(by).wait()
+        scales[...] += along[by]
+
+    scales[...] = lax.rsqrt(scales[...] / totals_of + 1e-05)
+
+    def fill(by):
+        target = lax.rem(me + by, owners)
+        row = scales[pl.ds(target, 1), :]
+        staged[by] = (gated_ref[target] * row).astype(jnp.bfloat16)
+
+    @pl.loop(1, owners)
+    def _(by):
+        fill(by)
+        block_copy(by).start()
+
+    fill(0)
+    mine = pltpu.make_async_copy(
+        staged.at[0],
+        out_ref.at[pl.ds(pl.multiple_of(me * channels, 16), channels), :],
+        kept,
+    )
+    mine.start()
+    mine.wait()
+
+    @pl.loop(1, owners)
+    def _(by):
+        block_copy(by).wait_send()
+        block_arrival(by).wait_recv()
 
 
 def shards(total_channels, streams, short_taps, pole_rates, residues, skip, gain):
@@ -152,16 +281,17 @@
         ],
         axis=1,
     )
+    at_once = 2 if groups % 2 == 0 else 1
     gated, sums = pl.pallas_call(
-        mix,
-        grid=(groups,),
+        functools.partial(mix, at_once),
+        grid=(groups // at_once,),
         in_specs=[
-            pl.BlockSpec((3, width, length), lambda g: (0, g, 0)),
-            pl.BlockSpec((1, 3, BLOCK), lambda g: (g, 0, 0)),
-            pl.BlockSpec((width, 4), lambda g: (g, 0)),
+            pl.BlockSpec((3, at_once * width, length), lambda g: (0, g, 0)),
+            pl.BlockSpec((at_once, 3, BLOCK), lambda g: (g, 0, 0)),
+            pl.BlockSpec((at_once * width, 4), lambda g: (g, 0)),
         ],
         out_specs=[
-            pl.BlockSpec((owners, width, own), lambda g: (0, g, 0)),
+            pl.BlockSpec((owners, at_once * width, own), lambda g: (0, g, 0)),
             pl.BlockSpec((owners, own), lambda g: (0, 0)),
         ],
         out_shape=[
@@ -171,10 +301,31 @@
         scratch_shapes=[pltpu.VMEM((length // BLOCK, 8, BLOCK), jnp.float32)],
         compiler_params=pltpu.CompilerParams(vmem_limit_bytes=48 * 1024 * 1024),
     )(streams, taps, columns)
-    mean_square = lax.psum(sums, ("ctx", "ch")) / total_channels
-    scaled = (gated * lax.rsqrt(mean_square + 1e-05)[:, None, :]).astype(jnp.bfloat16)
-    moved = lax.all_to_all(scaled, "ctx", split_axis=0, concat_axis=0, tiled=True)
-    return moved.reshape(owners * channels, own)
+    across = lax.axis_size("ch")
+    dma = pltpu.SemaphoreType.DMA
+    return pl.pallas_call(
+        functools.partial(send, total_channels),
+        in_specs=[pl.BlockSpec(memory_space=pltpu.VMEM)] * 2,
+        out_specs=pl.BlockSpec(memory_space=pl.ANY),
+        out_shape=jax.ShapeDtypeStruct((owners * channels, own), jnp.bfloat16),
+        scratch_shapes=[
+            pltpu.VMEM((across, owners, own), jnp.float32),
+            pltpu.VMEM((owners, own), jnp.float32),
+            pltpu.VMEM((owners, owners, own), jnp.float32),
+            pltpu.VMEM((owners, channels, own), jnp.bfloat16),
+            pltpu.VMEM((owners, own), jnp.float32),
+            dma((across,)),
+            dma((across,)),
+            dma((owners,)),
+            dma((owners,)),
+            dma((owners,)),
+            dma((owners,)),
+            dma,
+        ],
+        compiler_params=pltpu.CompilerParams(
+            collective_id=0, has_side_effects=True, vmem_limit_bytes=24 * 1024 * 1024
+        ),
+    )(sums, gated)
 
 
 def solution(mesh):

time: 98.3 us -> 58 us (0.59)
  the two profiles are of different devices: /device:TPU:0 before, /device:TPU:10 now
where the time goes in v2:
time: 58 us; the launch traced here: 57.7 us
  Pallas kernels  51.8 us (89%)
  local copies, waits for them, and re-layouts  5.81 us (10%)
    pallas_call x1, Pallas kernels, shards(): pl.pallas_call(functools.partial(send, total_channels), in_specs=[pl.Bloc...  34.6 us
    pallas_call x1, Pallas kernels, shards(): pl.pallas_call(functools.partial(mix, at_once), grid=(groups // at_once,)...  17.2 us
    unnamed x6, local copies, waits for them, and re-layouts  2.97 us

profile of v2, /device:TPU:10, one launch (start us, length us, event | category | flops | bytes accessed | tf_op | source)
XLA Modules:
  0.0 57.7 jit_solution(17123234959404722260)
XLA Ops:
  0.0 0.0 copy-start
  0.0 0.8 %dynamic_slice.16 = f32[256]{0:T(256)S(1)} dynamic-slice(f32[2048]{0:T(1024)} %param.10, s32[]{:T(128)S(6)} %select_n.10), dynamic_slice_sizes={256} | dynamic-slice | bytes 2052 | tf_op jit(solution)/shard_map/dynamic_slice | solution.py:277
  0.8 0.8 %dynamic_slice.17 = f32[256]{0:T(256)S(1)} dynamic-slice(f32[2048]{0:T(1024)} %param.11, s32[]{:T(128)S(6)} %select_n.10), dynamic_slice_sizes={256} | dynamic-slice | bytes 2052 | tf_op jit(solution)/shard_map/dynamic_slice | solution.py:278
  1.5 0.0 copy-done
  1.5 0.1 constant_dynamic-slice_fusion.2
  1.6 0.8 %constant_dynamic-slice_fusion = (f32[16,16]{0,1:T(8,128)S(1)}, f32[16,16]{0,1:T(8,128)S(1)}) fusion(f32[128,16]{0,1:T(8,128)} %param.9, s32[]{:T(128)S(6)} %select_n.4, f32[128,16]{0,1:T(8,128)} %param.8), kind=kLoop, calls=%fused_computation.1 | loop fusion | bytes 4100 | tf_op jit(solution)/shard_map/dynamic_slice | solution.py:280
  2.4 0.1 copy.19
  2.5 0.1 stack_reshape.7
  2.6 0.1 copy.18
  2.6 0.1 stack_reshape.6
  2.7 0.1 copy.21
  2.8 0.1 copy.20.columns_ref
  3.0 0.0 copy-start.1
  3.0 1.9 %copy-done.1 = bf16[3,256,2048]{2,1,0:T(8,128)(2,1)S(1)} copy-done((bf16[3,256,2048]{2,1,0:T(8,128)(2,1)S(1)}, bf16[3,256,2048]{2,1,0:T(8,128)(2,1)}, u32[]{:S(2)}) %copy-start.1) | copy-done | bytes 3145752
  4.9 17.2 %shard_map.64 = (f32[8,256,256]{2,1,0:T(8,128)S(1)}, f32[8,256]{1,0:T(8,128)S(1)}) custom-call(bf16[3,256,2048]{2,1,0:T(8,128)(2,1)S(1)} %copy-done.1, f32[16,3,128]{2,1,0:T(4,128)S(1)} %pad.4.taps_ref, f32[256,4]{1,0:T(8,128)S(1)} %copy.20.columns_ref), custom_call_target="tpu_custom_call" | custom-call | tf_op jit(solution)/shard_map/pallas_call | solution.py:285
  22.0 34.6 %shard_map.65 = bf16[2048,256]{1,0:T(8,128)(2,1)S(1)} custom-call(f32[8,256]{1,0:T(8,128)S(1)} %get-tuple-element.7.sums_ref, f32[8,256,256]{2,1,0:T(8,128)S(1)} %get-tuple-element.8.gated_ref), custom_call_target="tpu_custom_call" | custom-call | tf_op jit(solution)/shard_map/pallas_call | solution.py:306
  56.7 1.0 %copy.23 = bf16[2048,256]{1,0:T(8,128)(2,1)} copy(bf16[2048,256]{1,0:T(8,128)(2,1)S(1)} %shard_map.65) | data formatting | bytes 2097152
  (2 shorter events, 0.0 us)
Async XLA Ops:
  0.0 1.5 %copy-start = (f32[3,128,7]{1,2,0:T(8,128)S(1)}, f32[3,128,7]{1,2,0:T(8,128)}, u32[]{:S(2)}) copy-start(f32[3,128,7]{1,2,0:T(8,128)} %param.7) | copy-start | bytes 32260
  3.0 1.9 %copy-start.1 = (bf16[3,256,2048]{2,1,0:T(8,128)(2,1)S(1)}, bf16[3,256,2048]{2,1,0:T(8,128)(2,1)}, u32[]{:S(2)}) copy-start(bf16[3,256,2048]{2,1,0:T(8,128)(2,1)} %streams_ref.1) | copy-start | bytes 9437188

commit v3 on v0

v3 whole, which is shorter than its diff:
```python
import functools

import jax
import jax.numpy as jnp
from jax import lax
from jax.experimental import pallas as pl
from jax.experimental.pallas import tpu as pltpu
from jax.sharding import PartitionSpec as P

BLOCK = 128
MESH = pl.DeviceIdType.MESH


def split(value):
    high = value.astype(jnp.bfloat16)
    low = (value - high.astype(jnp.float32)).astype(jnp.bfloat16)
    return high, low


def halves(array):
    return array[:, :BLOCK] + array[:, BLOCK:]


def rolled(row):
    return pltpu.roll(
        jnp.broadcast_to(row, (BLOCK, BLOCK)), 0, 1, stride=1, stride_axis=0
    )


def column_of(row):
    shape = (row.shape[1], row.shape[1])
    diagonal = lax.broadcasted_iota(jnp.int32, shape, 0) == lax.broadcasted_iota(
        jnp.int32, shape, 1
    )
    return jnp.sum(jnp.where(diagonal, row, 0.0), axis=1, keepdims=True)


def causal_mask():
    shape = (BLOCK, BLOCK)
    return lax.broadcasted_iota(jnp.int32, shape, 1) >= lax.broadcasted_iota(jnp.int32, shape, 0)


def short_weights(taps_row):
    row = jnp.concatenate(
        [taps_row, jnp.zeros((1, BLOCK - taps_row.shape[1]), jnp.float32)], axis=1
    )
    table = rolled(row)
    causal = causal_mask()
    high_now, low_now = split(jnp.where(causal, table, 0.0))
    high_before, low_before = split(jnp.where(causal, 0.0, table))
    return jnp.concatenate(
        [
            jnp.concatenate([high_before, low_before], axis=1),
            jnp.concatenate([high_now, low_now], axis=1),
        ],
        axis=0,
    )


def short_filtered(window, m, rows, chosen, weights):
    def block_at(n):
        return window[m, rows, n * BLOCK : (n + 1) * BLOCK]

    now = jnp.concatenate([block_at(n) for n in chosen], axis=0)
    before = jnp.concatenate(
        [block_at(n - 1) if n else jnp.zeros_like(block_at(0)) for n in chosen], axis=0
    )
    both = jnp.concatenate([before, now], axis=1)
    return halves(jnp.dot(both, weights, preferred_element_type=jnp.float32))


def fused(
    total_channels,
    at_once,
    streams,
    taps,
    pole_rates,
    residues_of,
    skips,
    gains,
    out,
    window,
    gated_at,
    filters,
    tables,
    lifts,
    pairs,
    starts_at,
    squares,
    across,
    column,
    along,
    scales,
    staged,
    fetched,
    across_sent,
    across_got,
    along_sent,
    along_got,
    block_sent,
    block_got,
    kept,
):
    chunks, owners, channels, _ = gated_at.shape
    width = skips.shape[1]
    groups = channels // width
    steps = groups // at_once
    blocks = window.shape[2] // BLOCK
    across_count = lax.axis_size("ch")
    me = lax.axis_index("ctx")
    my_ch = lax.axis_index("ch")
    first_group = me * groups

    def fetch(step):
        rows = pl.ds(pl.multiple_of(step * (at_once * width), 16), at_once * width)
        return pltpu.make_async_copy(
            streams.at[:, rows, :], window.at[:, rows, :], fetched.at[step]
        )

    @pl.loop(0, steps)
    def _(step):
        fetch(step).start()

    def peer_ctx(by):
        return {"ctx": lax.rem(me + by, owners)}

    def peer_ch(by):
        return {"ch": lax.rem(my_ch + by, across_count)}

    barrier = pltpu.get_barrier_semaphore()

    @pl.loop(1, across_count)
    def _(by):
        pl.semaphore_signal(barrier, inc=1, device_id=peer_ch(by), device_id_type=MESH)

    @pl.loop(1, owners)
    def _(by):
        pl.semaphore_signal(barrier, inc=1, device_id=peer_ctx(by), device_id_type=MESH)

    def rows_of(group):
        return pl.ds(pl.multiple_of(group * width, 16), width)

    def finish(group, chunk, pair, starts):
        chosen = range(chunk, blocks, chunks)
        value = short_filtered(window, 0, rows_of(group), chosen, filters[group])
        summed = jnp.dot(pair, tables[group], preferred_element_type=jnp.float32)
        summed += jnp.dot(starts, lifts[group], preferred_element_type=jnp.float32)
        skip = column_of(skips[pl.ds(first_group + group, 1), :])
        gain = column_of(gains[pl.ds(first_group + group, 1), :])
        shaped = (owners, width, BLOCK)
        product = halves(pair.astype(jnp.float32)).reshape(shaped)
        gated = value.reshape(shaped) * (halves(summed).reshape(shaped) + skip[None] * product)
        gated_at[chunk, :, rows_of(group), :] = gated * gain[None]
        return jnp.sum((gated * gated).reshape(owners, width // 8, 8, BLOCK), axis=1)

    def begin(group):
        row = pl.ds(first_group + group, 1)
        filters[group] = short_weights(taps[0, row, :])
        product = 1.0
        for m in (1, 2):
            product *= short_filtered(
                window, m, rows_of(group), range(blocks), short_weights(taps[m, row, :])
            )
        high, low = split(product)
        pair = jnp.concatenate([high, low], axis=1)

        rates = column_of(pole_rates[row, :])
        residues = column_of(residues_of[row, :])
        lags = lax.broadcasted_iota(jnp.int32, (width, BLOCK), 1).astype(jnp.float32)
        modes = residues * jnp.exp(-rates * lags)
        table_high, table_low = split(
            jnp.where(causal_mask(), rolled(jnp.sum(modes, axis=0, keepdims=True)), 0.0)
        )
        table_row = jnp.concatenate([table_high, table_low], axis=1)
        tables[group] = jnp.concatenate([table_row, table_row], axis=0)
        lift_high, lift_low = split(residues * jnp.exp(-rates * (lags + 1.0)))
        lift_row = jnp.concatenate([lift_high, lift_low], axis=1)
        lifts[group] = jnp.concatenate([lift_row, lift_row], axis=0)

        back_high, back_low = split(jnp.exp(-rates * (BLOCK - 1 - lags)))
        back = jnp.concatenate(
            [
                jnp.concatenate([back_high, back_high], axis=1),
                jnp.concatenate([back_low, back_low], axis=1),
            ],
            axis=0,
        )
        ends = lax.dot_general(
            back, pair, (((1,), (1,)), ((), ())), preferred_element_type=jnp.float32
        )
        states = ends[:width] + ends[width:]
        lane = lax.broadcasted_iota(jnp.int32, states.shape, 1)
        reach = 1
        while reach < blocks:
            earlier = pltpu.roll(states, reach * width, 1)
            decay = jnp.exp(-rates * (BLOCK * reach))
            states = states + jnp.where(lane >= reach * width, decay * earlier, 0.0)
            reach *= 2
        starts = jnp.where(lane >= width, pltpu.roll(states, width, 1), 0.0)
        starts_high, starts_low = split(starts)
        starts = jnp.concatenate(
            [starts_high.astype(jnp.float32), starts_low.astype(jnp.float32)], axis=0
        ).T.astype(jnp.bfloat16)

        def of_chunk(array, chunk):
            return jnp.concatenate(
                [array[n * width : (n + 1) * width] for n in range(chunk, blocks, chunks)], axis=0
            )

        for chunk in range(1, chunks):
            pairs[chunk - 1, group] = of_chunk(pair, chunk)
            starts_at[chunk - 1, group] = of_chunk(starts, chunk)
        return of_chunk(pair, 0), of_chunk(starts, 0)

    squares[...] = jnp.zeros_like(squares)

    @pl.loop(0, steps)
    def _(step):
        fetch(step).wait()
        begun = [begin(step * at_once + i) for i in range(at_once)]
        for i, held in enumerate(begun):
            squares[0] += finish(step * at_once + i, 0, *held)

    def later(chunk, low, high):
        @pl.loop(low, high)
        def _(step):
            total = 0.0
            for i in range(at_once):
                group = step * at_once + i
                total += finish(
                    group, chunk, pairs[chunk - 1, group], starts_at[chunk - 1, group]
                )
            squares[chunk] += total

    def across_copy(chunk, by):
        return pltpu.make_async_remote_copy(
            src_ref=across.at[chunk, 0],
            dst_ref=across.at[chunk, by],
            send_sem=across_sent.at[chunk, by],
            recv_sem=across_got.at[chunk, by],
            device_id=peer_ch(by),
            device_id_type=MESH,
        )

    def along_copy(chunk, by):
        return pltpu.make_async_remote_copy(
            src_ref=column.at[chunk],
            dst_ref=along.at[chunk, by],
            send_sem=along_sent.at[chunk, by],
            recv_sem=along_got.at[chunk, by],
            device_id=peer_ctx(by),
            device_id_type=MESH,
        )

    def place(chunk, owner):
        return out.at[
            pl.ds(pl.multiple_of(owner * channels, 16), channels),
            chunk * BLOCK : (chunk + 1) * BLOCK,
        ]

    def block_copy(chunk, by, owner):
        return pltpu.make_async_remote_copy(
            src_ref=staged.at[chunk, by],
            dst_ref=place(chunk, owner),
            send_sem=block_sent.at[chunk, by],
            recv_sem=block_got.at[chunk, by],
            device_id=peer_ctx(by),
            device_id_type=MESH,
        )

    def start_across(chunk):
        across[chunk, 0] = jnp.sum(squares[chunk], axis=1)

        @pl.loop(1, across_count)
        def _(by):
            across_copy(chunk, by).start()

    def start_along(chunk):
        @pl.loop(1, across_count)
        def _(by):
            across_copy(chunk, by).wait()

        column[chunk] = jnp.sum(across[chunk], axis=0)

        @pl.loop(1, owners)
        def _(by):
            along_copy(chunk, by).start()

    def start_blocks(chunk):
        along[chunk, 0] = column[chunk]

        @pl.loop(1, owners)
        def _(by):
            along_copy(chunk, by).wait()

        total = jnp.sum(along[chunk], axis=0)
        scales[chunk] = lax.rsqrt(total / total_channels + 1e-05)

        def fill(by):
            target = lax.rem(me + by, owners)
            row = scales[chunk, pl.ds(target, 1), :]
            staged[chunk, by] = (gated_at[chunk, target] * row).astype(jnp.bfloat16)

        @pl.loop(1, owners)
        def _(by):
            fill(by)
            block_copy(chunk, by, me).start()

        fill(0)
        pltpu.make_async_copy(staged.at[chunk, 0], place(chunk, me), kept.at[chunk]).start()

    def wait_blocks(chunk):
        pltpu.make_async_copy(staged.at[chunk, 0], place(chunk, me), kept.at[chunk]).wait()

        @pl.loop(1, owners)
        def _(by):
            block_copy(chunk, by, me).wait_send()
            block_copy(chunk, by, lax.rem(me + owners - by, owners)).wait_recv()

    pl.semaphore_wait(barrier, across_count + owners - 2)
    cuts = (0, (3 * steps) // 8, (6 * steps) // 8, steps)
    for chunk in range(chunks):
        more = chunk + 1 < chunks
        start_across(chunk)
        if more:
            later(chunk + 1, cuts[0], cuts[1])
        start_along(chunk)
        if more:
            later(chunk + 1, cuts[1], cuts[2])
        start_blocks(chunk)
        if more:
            later(chunk + 1, cuts[2], cuts[3])
    for chunk in range(chunks):
        wait_blocks(chunk)


def shards(total_channels, streams, short_taps, pole_rates, residues, skip, gain):
    owners = lax.axis_size("ctx")
    across = lax.axis_size("ch")
    channels, length = streams.shape[1:]
    groups = pole_rates.shape[0] // owners
    width = channels // groups
    assert pole_rates.shape[1] == width
    own = length // owners
    chunks = own // BLOCK
    later = max(chunks - 1, 1)
    at_once = 2 if groups % 2 == 0 else 1
    vmem = pltpu.VMEM
    dma = pltpu.SemaphoreType.DMA
    f32 = jnp.float32
    bf16 = jnp.bfloat16
    return pl.pallas_call(
        functools.partial(fused, total_channels, at_once),
        in_specs=[pl.BlockSpec(memory_space=pl.ANY)] + [pl.BlockSpec(memory_space=vmem)] * 5,
        out_specs=pl.BlockSpec(memory_space=pl.ANY),
        out_shape=jax.ShapeDtypeStruct((owners * channels, own), bf16),
        scratch_shapes=[
            vmem(streams.shape, bf16),
            vmem((chunks, owners, channels, BLOCK), f32),
            vmem((groups, 2 * BLOCK, 2 * BLOCK), bf16),
            vmem((groups, 2 * BLOCK, 2 * BLOCK), bf16),
            vmem((groups, 2 * width, 2 * BLOCK), bf16),
            vmem((later, groups, owners * width, 2 * BLOCK), bf16),
            vmem((later, groups, owners * width, 2 * width), bf16),
            vmem((chunks, owners, 8, BLOCK), f32),
            vmem((chunks, across, owners, BLOCK), f32),
            vmem((chunks, owners, BLOCK), f32),
            vmem((chunks, owners, owners, BLOCK), f32),
            vmem((chunks, owners, BLOCK), f32),
            vmem((chunks, owners, channels, BLOCK), bf16),
            dma((groups // at_once,)),
            dma((chunks, across)),
            dma((chunks, across)),
            dma((chunks, owners)),
            dma((chunks, owners)),
            dma((chunks, owners)),
            dma((chunks, owners)),
            dma((chunks,)),
        ],
        compiler_params=pltpu.CompilerParams(
            collective_id=0, has_side_effects=True, vmem_limit_bytes=56 * 1024 * 1024
        ),
    )(
        streams,
        short_taps,
        pole_rates,
        residues,
        skip.reshape(-1, width),
        gain.reshape(-1, width),
    )


def solution(mesh):
    placed = (
        P(None, ("ch", "ctx"), None),
        P(None, "ch", None),
        P("ch", None),
        P("ch", None),
        P("ch"),
        P("ch"),
    )

    def whole(streams, *others):
        return jax.shard_map(
            functools.partial(shards, streams.shape[1]),
            mesh=mesh,
            in_specs=placed,
            out_specs=P("ch", "ctx"),
            check_vma=False,
        )(streams, *others)

    return whole
```

time: 256 us -> 56.3 us (0.22); the launches traced: 252 us -> 55.3 us
  waiting for transfers between devices: 106 us -> 0 us
  Pallas kernels: 0 us -> 45.9 us
  starting transfers between devices: 40.9 us -> 0 us
  local copies, waits for them, and re-layouts: 44.7 us -> 9.4 us
  matrix products: 28.2 us -> 0 us
  other arithmetic: 26 us -> 0 us
  blocking collectives: 5.66 us -> 0 us
    all_to_all x1 -> x0, waiting for transfers between devices: 78.2 us -> none  [shards(): lax.all_to_all(streams, 'ctx', split_axis=2, concat_axis=1, tiled=True)]
    pallas_call x0 -> x1, Pallas kernels: none -> 45.9 us  [shards(): pl.pallas_call(functools.partial(fused, total_channels, at_once), in_spec...]
    ppermute x8 -> x0, starting transfers between devices: 34.5 us -> none  [passed_along(): return lax.ppermute(array, axis, pairs)]
    dot_general x5 -> x0, matrix products: 28.2 us -> none  [the longest x1 16.8 us: block_terms(): jnp.einsum('gsnk,gik->gsni', current, kernel, precision=HIGHEST_PRECISION)]
    ppermute x8 -> x0, waiting for transfers between devices: 27.9 us -> none  [passed_along(): return lax.ppermute(array, axis, pairs)]
    add x9 -> x0, other arithmetic: 16.9 us -> none  [the longest x1 15.2 us: short_filter(): summed = summed + short_taps[:, :, offset][:, :, None, None] * window]
    unnamed x33 -> x4, local copies, waits for them, and re-layouts: 14.9 us -> 6.61 us
    all_to_all x2 -> x0, local copies, waits for them, and re-layouts: 7.44 us -> none  [shards(): lax.all_to_all(streams, 'ctx', split_axis=2, concat_axis=1, tiled=True)]
  transfers between devices with their start and end apart: 9 -> 0, of which waited for: 9 -> 0; matrix products, arithmetic and copies ran while one was open for 5% -> 0% of each run, Pallas kernels for 0% -> 0%
where the time goes in v3:
time: 56.3 us; the launch traced here: 55.3 us
  Pallas kernels  45.9 us (82%)
  local copies, waits for them, and re-layouts  9.4 us (17%)
    pallas_call x1, Pallas kernels, shards(): pl.pallas_call(functools.partial(fused, total_channels, at_once), in_spec...  45.9 us
    unnamed x4, local copies, waits for them, and re-layouts  6.61 us
    reshape x1, local copies, waits for them, and re-layouts, shards(): skip.reshape(-1, width)  1.4 us
    reshape x1, local copies, waits for them, and re-layouts, shards(): gain.reshape(-1, width)  1.39 us

profile of v3, /device:TPU:10, one launch (start us, length us, event | category | flops | bytes accessed | tf_op | source)
XLA Modules:
  0.0 55.3 jit_solution(11573239984351897065)
XLA Ops:
  0.0 1.4 %copy.11.pole_rates = f32[128,16]{1,0:T(8,128)} copy(f32[128,16]{0,1:T(8,128)} %param.8) | data formatting | bytes 16384 | tf_op args[2]
  1.4 1.4 %copy.12.residues_of = f32[128,16]{1,0:T(8,128)} copy(f32[128,16]{0,1:T(8,128)} %param.9) | data formatting | bytes 16384 | tf_op args[3]
  2.8 1.4 %reshape.6.skips = f32[128,16]{1,0:T(8,128)} reshape(f32[2048]{0:T(1024)} %param.10) | data formatting | bytes 16384 | tf_op jit(solution)/shard_map/reshape | solution.py:388
  4.2 1.4 %reshape.7.gains = f32[128,16]{1,0:T(8,128)} reshape(f32[2048]{0:T(1024)} %param.11) | data formatting | bytes 16384 | tf_op jit(solution)/shard_map/reshape | solution.py:389
  5.6 1.5 %copy.10.taps = f32[3,128,7]{2,1,0:T(8,128)} copy(f32[3,128,7]{1,2,0:T(8,128)} %param.7) | data formatting | bytes 21504 | tf_op args[1]
  7.1 45.9 %shard_map.64 = bf16[2048,256]{1,0:T(8,128)(2,1)} custom-call(bf16[3,256,2048]{2,1,0:T(8,128)(2,1)} %streams.1, f32[3,128,7]{2,1,0:T(8,128)} %copy.10.taps, f32[128,16]{1,0:T(8,128)} %copy.11.pole_rates, f32[128,16]{1,0:T(8,128)} %copy.12.residues_of, f32[128,16]{1,0:T(8,128)} %reshape.6.skips, f32[128,16]{1,0:T(8,128)} %reshape.7.gains), custom_call_target="tpu_custom_call" | custom-call | tf_op jit(solution)/shard_map/pallas_call | solution.py:352
  53.0 2.3 %copy.14 = bf16[2048,256]{1,0:T(8,128)(2,1)} copy(bf16[2048,256]{1,0:T(8,128)(2,1)} %shard_map.64) | data formatting | bytes 2097152

commit v4 on v3

v4 whole, which is shorter than its diff:
```python
import functools

import jax
import jax.numpy as jnp
from jax import lax
from jax.experimental import pallas as pl
from jax.experimental.pallas import tpu as pltpu
from jax.sharding import PartitionSpec as P

BLOCK = 128
MESH = pl.DeviceIdType.MESH


def split(value):
    high = value.astype(jnp.bfloat16)
    low = (value - high.astype(jnp.float32)).astype(jnp.bfloat16)
    return high, low


def halves(array):
    return array[:, :BLOCK] + array[:, BLOCK:]


def rolled(row):
    return pltpu.roll(
        jnp.broadcast_to(row, (BLOCK, BLOCK)), 0, 1, stride=1, stride_axis=0
    )


def picked(array, lane):
    lanes = lax.broadcasted_iota(jnp.int32, array.shape, 1)
    return jnp.sum(jnp.where(lanes == lane, array, 0.0), axis=1, keepdims=True)


def upright(row, offset, width):
    shape = (width, row.shape[1])
    lane = lax.broadcasted_iota(jnp.int32, shape, 1)
    at = lax.broadcasted_iota(jnp.int32, shape, 0) + offset
    return jnp.sum(jnp.where(lane == at, row, 0.0), axis=1, keepdims=True)


def flat(column):
    shape = (column.shape[0], BLOCK)
    diagonal = lax.broadcasted_iota(jnp.int32, shape, 0) == lax.broadcasted_iota(
        jnp.int32, shape, 1
    )
    return jnp.sum(jnp.where(diagonal, column, 0.0), axis=0, keepdims=True)


def causal_mask():
    shape = (BLOCK, BLOCK)
    row = lax.broadcasted_iota(jnp.int32, shape, 0)
    lane = lax.broadcasted_iota(jnp.int32, shape, 1)
    return jnp.where(lane >= row, 1.0, 0.0).astype(jnp.bfloat16)


def short_weights(taps_column, causal):
    high, low = split(rolled(flat(taps_column)))
    now = jnp.concatenate([high * causal, low * causal], axis=1)
    before = jnp.concatenate([high, low], axis=1) - now
    return jnp.concatenate([before, now], axis=0)


def short_filtered(window, m, rows, chosen, weights):
    def block_at(n):
        return window[m, rows, n * BLOCK : (n + 1) * BLOCK]

    now = jnp.concatenate([block_at(n) for n in chosen], axis=0)
    before = jnp.concatenate(
        [block_at(n - 1) if n else jnp.zeros_like(block_at(0)) for n in chosen], axis=0
    )
    both = jnp.concatenate([before, now], axis=1)
    return halves(jnp.dot(both, weights, preferred_element_type=jnp.float32))


def fused(
    total_channels,
    at_once,
    streams,
    taps,
    pole_rates,
    residues_of,
    skips,
    gains,
    out,
    window,
    gated_at,
    filters,
    tables,
    held_at,
    squares,
    sums,
    scales,
    staged,
    fetched,
    sums_sent,
    sums_got,
    block_sent,
    block_got,
    kept,
):
    chunks, owners, channels, _ = gated_at.shape
    width = pole_rates.shape[0]
    groups = channels // width
    steps = groups // at_once
    blocks = window.shape[2] // BLOCK
    across_count = lax.axis_size("ch")
    me = lax.axis_index("ctx")
    my_ch = lax.axis_index("ch")
    first_group = me * groups

    def fetch(step):
        rows = pl.ds(pl.multiple_of(step * (at_once * width), 16), at_once * width)
        return pltpu.make_async_copy(
            streams.at[:, rows, :], window.at[:, rows, :], fetched.at[step]
        )

    @pl.loop(0, steps)
    def _(step):
        fetch(step).start()

    def peer_ctx(by):
        return {"ctx": lax.rem(me + by, owners)}

    def peer(by):
        return {
            "ctx": lax.rem(me + lax.div(by, across_count), owners),
            "ch": lax.rem(my_ch + lax.rem(by, across_count), across_count),
        }

    devices = owners * across_count
    barrier = pltpu.get_barrier_semaphore()

    @pl.loop(1, devices)
    def _(by):
        pl.semaphore_signal(barrier, inc=1, device_id=peer(by), device_id_type=MESH)

    causal = causal_mask()

    def rows_of(group):
        return pl.ds(pl.multiple_of(group * width, 16), width)

    def per_channel(values, group):
        at = (first_group + group) * width
        return upright(values[pl.ds(lax.div(at, BLOCK), 1), :], lax.rem(at, BLOCK), width)

    def finish(group, chunk, held):
        chosen = range(chunk, blocks, chunks)
        value = short_filtered(window, 0, rows_of(group), chosen, filters[group])
        high, low, starts = (held[:, i * BLOCK : (i + 1) * BLOCK] for i in range(3))
        convolved = jnp.dot(
            jnp.concatenate([high, low, high, starts], axis=1),
            tables[group],
            preferred_element_type=jnp.float32,
        )
        skip = per_channel(skips, group)
        gain = per_channel(gains, group)
        shaped = (owners, width, BLOCK)
        product = (high.astype(jnp.float32) + low.astype(jnp.float32)).reshape(shaped)
        gated = value.reshape(shaped) * (convolved.reshape(shaped) + skip[None] * product)
        gated_at[chunk, :, rows_of(group), :] = gated * gain[None]
        return jnp.sum((gated * gated).reshape(owners, width // 8, 8, BLOCK), axis=1)

    def begin(group):
        at = first_group + group
        filters[group] = short_weights(picked(taps[0], at), causal)
        product = 1.0
        for m in (1, 2):
            product *= short_filtered(
                window, m, rows_of(group), range(blocks), short_weights(picked(taps[m], at), causal)
            )
        high, low = split(product)
        pair = jnp.concatenate([high, low], axis=1)

        rates = picked(pole_rates[...], at)
        residues = picked(residues_of[...], at)
        lags = lax.broadcasted_iota(jnp.int32, (width, BLOCK), 1).astype(jnp.float32)
        modes = residues * jnp.exp(-rates * lags)
        table_high, table_low = split(rolled(jnp.sum(modes, axis=0, keepdims=True)))
        table_high = table_high * causal
        lift_high, lift_low = split(residues * jnp.exp(-rates * (lags + 1.0)))
        spare = BLOCK - 3 * width
        tables[group] = jnp.concatenate(
            [
                table_high,
                table_high,
                table_low * causal,
                lift_high,
                lift_high,
                lift_low,
                jnp.zeros((spare, BLOCK), jnp.bfloat16),
            ],
            axis=0,
        )

        back_high, back_low = split(jnp.exp(-rates * (BLOCK - 1 - lags)))
        back = jnp.concatenate(
            [
                jnp.concatenate([back_high, back_high], axis=1),
                jnp.concatenate([back_low, back_low], axis=1),
            ],
            axis=0,
        )
        ends = lax.dot_general(
            back, pair, (((1,), (1,)), ((), ())), preferred_element_type=jnp.float32
        )
        states = ends[:width] + ends[width:]
        lane = lax.broadcasted_iota(jnp.int32, states.shape, 1)
        reach = 1
        while reach < blocks:
            earlier = pltpu.roll(states, reach * width, 1)
            decay = jnp.exp(-rates * (BLOCK * reach))
            states = states + jnp.where(lane >= reach * width, decay * earlier, 0.0)
            reach *= 2
        starts = jnp.where(lane >= width, pltpu.roll(states, width, 1), 0.0)
        starts_high, starts_low = (part.astype(jnp.float32) for part in split(starts))
        starts = jnp.concatenate(
            [
                starts_high,
                starts_low,
                starts_high,
                jnp.zeros((spare, starts.shape[1]), jnp.float32),
            ],
            axis=0,
        ).T.astype(jnp.bfloat16)
        held = jnp.concatenate([pair, starts], axis=1)

        def of_chunk(chunk):
            return jnp.concatenate(
                [held[n * width : (n + 1) * width] for n in range(chunk, blocks, chunks)], axis=0
            )

        for chunk in range(1, chunks):
            held_at[chunk - 1, group] = of_chunk(chunk)
        return of_chunk(0)

    squares[...] = jnp.zeros_like(squares)

    @pl.loop(0, steps)
    def _(step):
        fetch(step).wait()
        begun = [begin(step * at_once + i) for i in range(at_once)]
        for i, held in enumerate(begun):
            squares[0] += finish(step * at_once + i, 0, held)

    def later(chunk, low, high):
        @pl.loop(low, high)
        def _(step):
            total = 0.0
            for i in range(at_once):
                group = step * at_once + i
                total += finish(group, chunk, held_at[chunk - 1, group])
            squares[chunk] += total

    def sums_copy(chunk, by):
        return pltpu.make_async_remote_copy(
            src_ref=sums.at[chunk, 0],
            dst_ref=sums.at[chunk, by],
            send_sem=sums_sent.at[chunk, by],
            recv_sem=sums_got.at[chunk, by],
            device_id=peer(by),
            device_id_type=MESH,
        )

    def place(chunk, owner):
        return out.at[
            pl.ds(pl.multiple_of(owner * channels, 16), channels),
            chunk * BLOCK : (chunk + 1) * BLOCK,
        ]

    def block_copy(chunk, by, owner):
        return pltpu.make_async_remote_copy(
            src_ref=staged.at[chunk, by],
            dst_ref=place(chunk, owner),
            send_sem=block_sent.at[chunk, by],
            recv_sem=block_got.at[chunk, by],
            device_id=peer_ctx(by),
            device_id_type=MESH,
        )

    def start_sums(chunk):
        sums[chunk, 0] = jnp.sum(squares[chunk], axis=1)

        @pl.loop(1, devices)
        def _(by):
            sums_copy(chunk, by).start()

    def start_blocks(chunk):
        @pl.loop(1, devices)
        def _(by):
            sums_copy(chunk, by).wait()

        total = jnp.sum(sums[chunk], axis=0)
        scales[chunk] = lax.rsqrt(total / total_channels + 1e-05)

        def fill(by):
            target = lax.rem(me + by, owners)
            row = scales[chunk, pl.ds(target, 1), :]
            staged[chunk, by] = (gated_at[chunk, target] * row).astype(jnp.bfloat16)

        @pl.loop(1, owners)
        def _(by):
            fill(by)
            block_copy(chunk, by, me).start()

        fill(0)
        pltpu.make_async_copy(staged.at[chunk, 0], place(chunk, me), kept.at[chunk]).start()

    def wait_blocks(chunk):
        pltpu.make_async_copy(staged.at[chunk, 0], place(chunk, me), kept.at[chunk]).wait()

        @pl.loop(1, owners)
        def _(by):
            block_copy(chunk, by, me).wait_send()
            block_copy(chunk, by, lax.rem(me + owners - by, owners)).wait_recv()

    pl.semaphore_wait(barrier, devices - 1)
    start_sums(0)
    for chunk in range(chunks):
        if chunk + 1 < chunks:
            later(chunk + 1, 0, steps)
            start_sums(chunk + 1)
        start_blocks(chunk)
    for chunk in range(chunks):
        wait_blocks(chunk)


def shards(total_channels, streams, short_taps, pole_rates, residues, skip, gain):
    owners = lax.axis_size("ctx")
    across = lax.axis_size("ch")
    channels, length = streams.shape[1:]
    groups = pole_rates.shape[0] // owners
    width = channels // groups
    assert pole_rates.shape[1] == width
    own = length // owners
    chunks = own // BLOCK
    later = max(chunks - 1, 1)
    devices = owners * across
    at_once = 2 if groups % 2 == 0 else 1
    vmem = pltpu.VMEM
    dma = pltpu.SemaphoreType.DMA
    f32 = jnp.float32
    bf16 = jnp.bfloat16
    return pl.pallas_call(
        functools.partial(fused, total_channels, at_once),
        in_specs=[pl.BlockSpec(memory_space=pltpu.HBM)] + [pl.BlockSpec(memory_space=vmem)] * 5,
        out_specs=pl.BlockSpec(memory_space=pl.ANY),
        out_shape=jax.ShapeDtypeStruct((owners * channels, own), bf16),
        scratch_shapes=[
            vmem(streams.shape, bf16),
            vmem((chunks, owners, channels, BLOCK), f32),
            vmem((groups, 2 * BLOCK, 2 * BLOCK), bf16),
            vmem((groups, 4 * BLOCK, BLOCK), bf16),
            vmem((later, groups, owners * width, 3 * BLOCK), bf16),
            vmem((chunks, owners, 8, BLOCK), f32),
            vmem((chunks, devices, owners, BLOCK), f32),
            vmem((chunks, owners, BLOCK), f32),
            vmem((chunks, owners, channels, BLOCK), bf16),
            dma((groups // at_once,)),
            dma((chunks, devices)),
            dma((chunks, devices)),
            dma((chunks, owners)),
            dma((chunks, owners)),
            dma((chunks,)),
        ],
        compiler_params=pltpu.CompilerParams(
            collective_id=0, has_side_effects=True, vmem_limit_bytes=40 * 1024 * 1024
        ),
    )(
        streams,
        short_taps.transpose(0, 2, 1),
        pole_rates.T,
        residues.T,
        skip.reshape(-1, BLOCK),
        gain.reshape(-1, BLOCK),
    )


def solution(mesh):
    placed = (
        P(None, ("ch", "ctx"), None),
        P(None, "ch", None),
        P("ch", None),
        P("ch", None),
        P("ch"),
        P("ch"),
    )

    def whole(streams, *others):
        return jax.shard_map(
            functools.partial(shards, streams.shape[1]),
            mesh=mesh,
            in_specs=placed,
            out_specs=P("ch", "ctx"),
            check_vma=False,
        )(streams, *others)

    return whole
```

time: 56.3 us -> 51.4 us (0.913)
  local copies, waits for them, and re-layouts: 9.4 us -> 6.35 us
  Pallas kernels: 45.9 us -> 44.6 us
    reshape x2 -> x0, local copies, waits for them, and re-layouts: 2.79 us -> none  [the longest x1 1.4 us: shards(): skip.reshape(-1, width)]
    pallas_call x1, Pallas kernels: 45.9 us -> 44.6 us  [shards(): pl.pallas_call(functools.partial(fused, total_channels, at_once), in_spec...]
    unnamed x4 -> x13, local copies, waits for them, and re-layouts: 6.61 us -> 6.35 us
where the time goes in v4:
time: 51.4 us; the launch traced here: 50.9 us
  Pallas kernels  44.6 us (87%)
  local copies, waits for them, and re-layouts  6.35 us (12%)
    pallas_call x1, Pallas kernels, shards(): pl.pallas_call(functools.partial(fused, total_channels, at_once), in_spec...  44.6 us
    unnamed x13, local copies, waits for them, and re-layouts  6.35 us

profile of v4, /device:TPU:10, one launch (start us, length us, event | category | flops | bytes accessed | tf_op | source)
XLA Modules:
  0.0 50.9 jit_solution(8019475620945128173)
XLA Ops:
  0.0 0.0 copy-start
  0.0 1.9 %copy-done = bf16[3,256,2048]{2,1,0:T(8,128)(2,1)S(1)} copy-done((bf16[3,256,2048]{2,1,0:T(8,128)(2,1)S(1)}, bf16[3,256,2048]{2,1,0:T(8,128)(2,1)}, u32[]{:S(2)}) %copy-start) | copy-done | bytes 3145752
  1.9 0.0 copy-start.1
  1.9 0.7 %copy-done.1 = f32[3,128,7]{1,2,0:T(8,128)S(1)} copy-done((f32[3,128,7]{1,2,0:T(8,128)S(1)}, f32[3,128,7]{1,2,0:T(8,128)}, u32[]{:S(2)}) %copy-start.1) | copy-done | bytes 10776
  2.6 0.0 copy-start.2
  2.6 0.7 %copy-done.2 = f32[128,16]{0,1:T(8,128)S(1)} copy-done((f32[128,16]{0,1:T(8,128)S(1)}, f32[128,16]{0,1:T(8,128)}, u32[]{:S(2)}) %copy-start.2) | copy-done | bytes 8216
  3.3 0.0 copy-start.3
  3.3 0.7 %copy-done.3 = f32[128,16]{0,1:T(8,128)S(1)} copy-done((f32[128,16]{0,1:T(8,128)S(1)}, f32[128,16]{0,1:T(8,128)}, u32[]{:S(2)}) %copy-start.3) | copy-done | bytes 8216
  4.0 0.0 copy-start.4
  4.0 0.7 %copy-done.4 = f32[2048]{0:T(1024)S(1)} copy-done((f32[2048]{0:T(1024)S(1)}, f32[2048]{0:T(1024)}, u32[]{:S(2)}) %copy-start.4) | copy-done | bytes 8216
  4.7 0.0 copy-start.5
  4.7 0.7 %copy-done.5 = f32[2048]{0:T(1024)S(1)} copy-done((f32[2048]{0:T(1024)S(1)}, f32[2048]{0:T(1024)}, u32[]{:S(2)}) %copy-start.5) | copy-done | bytes 8216
  5.4 44.6 %shard_map.64 = bf16[2048,256]{1,0:T(8,128)(2,1)S(1)} custom-call(bf16[3,256,2048]{2,1,0:T(8,128)(2,1)S(1)} %copy-done, f32[3,7,128]{2,1,0:T(8,128)S(1)} %bitcast.5, f32[16,128]{1,0:T(8,128)S(1)} %bitcast.6, f32[16,128]{1,0:T(8,128)S(1)} %bitcast.7, f32[16,128]{1,0:T(8,128)S(1)} %bitcast.8, f32[16,128]{1,0:T(8,128)S(1)} %bitcast.9), custom_call_target="tpu_custom_call" | custom-call | tf_op jit(solution)/shard_map/pallas_call | solution.py:344
  50.0 1.0 %copy.8 = bf16[2048,256]{1,0:T(8,128)(2,1)} copy(bf16[2048,256]{1,0:T(8,128)(2,1)S(1)} %shard_map.64) | data formatting | bytes 2097152
Async XLA Ops:
  0.0 1.9 %copy-start = (bf16[3,256,2048]{2,1,0:T(8,128)(2,1)S(1)}, bf16[3,256,2048]{2,1,0:T(8,128)(2,1)}, u32[]{:S(2)}) copy-start(bf16[3,256,2048]{2,1,0:T(8,128)(2,1)} %streams.1) | copy-start | bytes 9437188
  1.9 0.7 %copy-start.1 = (f32[3,128,7]{1,2,0:T(8,128)S(1)}, f32[3,128,7]{1,2,0:T(8,128)}, u32[]{:S(2)}) copy-start(f32[3,128,7]{1,2,0:T(8,128)} %param.7) | copy-start | bytes 32260
  2.6 0.7 %copy-start.2 = (f32[128,16]{0,1:T(8,128)S(1)}, f32[128,16]{0,1:T(8,128)}, u32[]{:S(2)}) copy-start(f32[128,16]{0,1:T(8,128)} %param.8) | copy-start | bytes 24580
  3.3 0.7 %copy-start.3 = (f32[128,16]{0,1:T(8,128)S(1)}, f32[128,16]{0,1:T(8,128)}, u32[]{:S(2)}) copy-start(f32[128,16]{0,1:T(8,128)} %param.9) | copy-start | bytes 24580
  4.0 0.7 %copy-start.4 = (f32[2048]{0:T(1024)S(1)}, f32[2048]{0:T(1024)}, u32[]{:S(2)}) copy-start(f32[2048]{0:T(1024)} %param.10) | copy-start | bytes 24580
  4.7 0.7 %copy-start.5 = (f32[2048]{0:T(1024)S(1)}, f32[2048]{0:T(1024)}, u32[]{:S(2)}) copy-start(f32[2048]{0:T(1024)} %param.11) | copy-start | bytes 24580

commit v5 on v4

--- a/solution.py
+++ b/solution.py
@@ -73,9 +73,24 @@
     return halves(jnp.dot(both, weights, preferred_element_type=jnp.float32))
 
 
+def settle(source, target, copied):
+    count = copied.shape[0]
+    height = source.shape[0] // count
+
+    def piece(i):
+        rows = pl.ds(i * height, height)
+        return pltpu.make_async_copy(source.at[rows, :], target.at[rows, :], copied.at[i])
+
+    for i in range(count):
+        piece(i).start()
+    for i in range(count):
+        piece(i).wait()
+
+
 def fused(
     total_channels,
     at_once,
+    early_steps,
     streams,
     taps,
     pole_rates,
@@ -92,7 +107,12 @@
     sums,
     scales,
     staged,
+    early,
+    early_staged,
     fetched,
+    early_sent,
+    early_got,
+    early_kept,
     sums_sent,
     sums_got,
     block_sent,
@@ -234,6 +254,36 @@
             held_at[chunk - 1, group] = of_chunk(chunk)
         return of_chunk(0)
 
+    early_channels = early_steps * at_once * width
+
+    def early_copy(step, by):
+        rows = pl.ds(pl.multiple_of(step * (at_once * width), 16), at_once * width)
+        return pltpu.make_async_remote_copy(
+            src_ref=gated_at.at[0, lax.rem(me + by, owners), rows, :],
+            dst_ref=early.at[by, rows, :],
+            send_sem=early_sent.at[step, by],
+            recv_sem=early_got.at[step, by],
+            device_id=peer_ctx(by),
+            device_id_type=MESH,
+        )
+
+    def early_keep(by):
+        source = lax.rem(me + owners - by, owners)
+        return pltpu.make_async_copy(
+            early_staged.at[by],
+            out.at[pl.ds(pl.multiple_of(source * channels, 16), early_channels), :BLOCK],
+            early_kept.at[by],
+        )
+
+    def keep_early():
+        @pl.loop(1, owners)
+        def _(by):
+            for step in range(early_steps):
+                early_copy(step, by).wait()
+            row = scales[0, pl.ds(me, 1), :]
+            early_staged[by] = (early[by] * row).astype(jnp.bfloat16)
+            early_keep(by).start()
+
     squares[...] = jnp.zeros_like(squares)
 
     @pl.loop(0, steps)
@@ -242,6 +292,18 @@
         begun = [begin(step * at_once + i) for i in range(at_once)]
         for i, held in enumerate(begun):
             squares[0] += finish(step * at_once + i, 0, held)
+
+        if early_steps:
+
+            @pl.when(step == 0)
+            def _():
+                pl.semaphore_wait(barrier, devices - 1)
+
+            @pl.when(step < early_steps)
+            def _():
+                @pl.loop(1, owners)
+                def _(by):
+                    early_copy(step, by).start()
 
     def later(chunk, low, high):
         @pl.loop(low, high)
@@ -262,22 +324,31 @@
             device_id_type=MESH,
         )
 
-    def place(chunk, owner):
+    def place(chunk, owner, first):
         return out.at[
-            pl.ds(pl.multiple_of(owner * channels, 16), channels),
+            pl.ds(pl.multiple_of(owner * channels + first, 16), channels - first),
             chunk * BLOCK : (chunk + 1) * BLOCK,
         ]
 
+    def first_of(chunk):
+        return early_channels if chunk == 0 else 0
+
     def block_copy(chunk, by, owner):
+        first = first_of(chunk)
         return pltpu.make_async_remote_copy(
-            src_ref=staged.at[chunk, by],
-            dst_ref=place(chunk, owner),
+            src_ref=staged.at[chunk, by, first:, :],
+            dst_ref=place(chunk, owner, first),
             send_sem=block_sent.at[chunk, by],
             recv_sem=block_got.at[chunk, by],
             device_id=peer_ctx(by),
             device_id_type=MESH,
         )
 
+    def own_copy(chunk):
+        return pltpu.make_async_copy(
+            staged.at[chunk, 0], place(chunk, me, 0), kept.at[chunk]
+        )
+
     def start_sums(chunk):
         sums[chunk, 0] = jnp.sum(squares[chunk], axis=1)
 
@@ -293,36 +364,46 @@
         total = jnp.sum(sums[chunk], axis=0)
         scales[chunk] = lax.rsqrt(total / total_channels + 1e-05)
 
-        def fill(by):
+        def fill(by, first):
             target = lax.rem(me + by, owners)
             row = scales[chunk, pl.ds(target, 1), :]
-            staged[chunk, by] = (gated_at[chunk, target] * row).astype(jnp.bfloat16)
+            staged[chunk, by, first:, :] = (gated_at[chunk, target, first:, :] * row).astype(
+                jnp.bfloat16
+            )
 
         @pl.loop(1, owners)
         def _(by):
-            fill(by)
+            fill(by, first_of(chunk))
             block_copy(chunk, by, me).start()
 
-        fill(0)
-        pltpu.make_async_copy(staged.at[chunk, 0], place(chunk, me), kept.at[chunk]).start()
+        fill(0, 0)
+        own_copy(chunk).start()
 
     def wait_blocks(chunk):
-        pltpu.make_async_copy(staged.at[chunk, 0], place(chunk, me), kept.at[chunk]).wait()
+        own_copy(chunk).wait()
 
         @pl.loop(1, owners)
         def _(by):
             block_copy(chunk, by, me).wait_send()
             block_copy(chunk, by, lax.rem(me + owners - by, owners)).wait_recv()
 
-    pl.semaphore_wait(barrier, devices - 1)
+    if not early_steps:
+        pl.semaphore_wait(barrier, devices - 1)
     start_sums(0)
     for chunk in range(chunks):
         if chunk + 1 < chunks:
             later(chunk + 1, 0, steps)
             start_sums(chunk + 1)
         start_blocks(chunk)
+    if early_steps:
+        keep_early()
     for chunk in range(chunks):
         wait_blocks(chunk)
+    if early_steps:
+
+        @pl.loop(1, owners)
+        def _(by):
+            early_keep(by).wait()
 
 
 def shards(total_channels, streams, short_taps, pole_rates, residues, skip, gain):
@@ -336,13 +417,16 @@
     chunks = own // BLOCK
     later = max(chunks - 1, 1)
     devices = owners * across
-    at_once = 2 if groups % 2 == 0 else 1
+    at_once = next(n for n in (4, 2, 1) if groups % n == 0)
+    steps = groups // at_once
+    early_steps = steps // 2
+    early_channels = max(early_steps, 1) * at_once * width
     vmem = pltpu.VMEM
     dma = pltpu.SemaphoreType.DMA
     f32 = jnp.float32
     bf16 = jnp.bfloat16
-    return pl.pallas_call(
-        functools.partial(fused, total_channels, at_once),
+    moved = pl.pallas_call(
+        functools.partial(fused, total_channels, at_once, early_steps),
         in_specs=[pl.BlockSpec(memory_space=pltpu.HBM)] + [pl.BlockSpec(memory_space=vmem)] * 5,
         out_specs=pl.BlockSpec(memory_space=pl.ANY),
         out_shape=jax.ShapeDtypeStruct((owners * channels, own), bf16),
@@ -356,7 +440,12 @@
             vmem((chunks, devices, owners, BLOCK), f32),
             vmem((chunks, owners, BLOCK), f32),
             vmem((chunks, owners, channels, BLOCK), bf16),
-            dma((groups // at_once,)),
+            vmem((owners, early_channels, BLOCK), f32),
+            vmem((owners, early_channels, BLOCK), bf16),
+            dma((steps,)),
+            dma((max(early_steps, 1), owners)),
+            dma((max(early_steps, 1), owners)),
+            dma((owners,)),
             dma((chunks, devices)),
             dma((chunks, devices)),
             dma((chunks, owners)),
@@ -364,7 +453,7 @@
             dma((chunks,)),
         ],
         compiler_params=pltpu.CompilerParams(
-            collective_id=0, has_side_effects=True, vmem_limit_bytes=40 * 1024 * 1024
+            collective_id=0, has_side_effects=True, vmem_limit_bytes=56 * 1024 * 1024
         ),
     )(
         streams,
@@ -374,6 +463,14 @@
         skip.reshape(-1, BLOCK),
         gain.reshape(-1, BLOCK),
     )
+    return pl.pallas_call(
+        settle,
+        in_specs=[pl.BlockSpec(memory_space=pl.ANY)],
+        out_specs=pl.BlockSpec(memory_space=pl.ANY),
+        out_shape=jax.ShapeDtypeStruct(moved.shape, moved.dtype),
+        scratch_shapes=[dma((8,))],
+        compiler_params=pltpu.CompilerParams(vmem_limit_bytes=56 * 1024 * 1024),
+    )(moved)
 
 
 def solution(mesh):

time: 51.4 us -> 77.6 us (1.51)
  Pallas kernels: 44.6 us -> 76.9 us
  local copies, waits for them, and re-layouts: 6.35 us -> 0 us
    pallas_call x1 -> x2, Pallas kernels: 44.6 us -> 76.9 us  [the longest x1 43.9 us: shards(): pl.pallas_call(functools.partial(fused, total_channels, at_once, early_st...]
    unnamed x13 -> x0, local copies, waits for them, and re-layouts: 6.35 us -> none
where the time goes in v5:
time: 77.6 us; the launch traced here: 76.9 us
  Pallas kernels  76.9 us (99%)
    pallas_call x1, Pallas kernels, shards(): pl.pallas_call(functools.partial(fused, total_channels, at_once, early_st...  43.9 us
    pallas_call x1, Pallas kernels, shards(): pl.pallas_call(settle, in_specs=[pl.BlockSpec(memory_space=pl.ANY)], out_...  32.9 us

profile of v5, /device:TPU:10, one launch (start us, length us, event | category | flops | bytes accessed | tf_op | source)
XLA Modules:
  0.0 76.9 jit_solution(14653998333308768252)
XLA Ops:
  0.0 43.9 %shard_map.64.source = bf16[2048,256]{1,0:T(8,128)(2,1)} custom-call(bf16[3,256,2048]{2,1,0:T(8,128)(2,1)} %streams.1, f32[3,7,128]{2,1,0:T(8,128)} %bitcast.5, f32[16,128]{1,0:T(8,128)} %bitcast.6, f32[16,128]{1,0:T(8,128)} %bitcast.7, f32[16,128]{1,0:T(8,128)} %bitcast.8, f32[16,128]{1,0:T(8,128)} %bitcast.9), custom_call_target="tpu_custom_call" | custom-call | tf_op jit(solution)/shard_map/pallas_call | solution.py:428
  44.0 32.9 %shard_map.65 = bf16[2048,256]{1,0:T(8,128)(2,1)} custom-call(bf16[2048,256]{1,0:T(8,128)(2,1)} %shard_map.64.source), custom_call_target="tpu_custom_call" | custom-call | tf_op jit(solution)/shard_map/pallas_call | solution.py:466

commit v6 on v5

--- a/solution.py
+++ b/solution.py
@@ -73,18 +73,31 @@
     return halves(jnp.dot(both, weights, preferred_element_type=jnp.float32))
 
 
-def settle(source, target, copied):
-    count = copied.shape[0]
-    height = source.shape[0] // count
-
-    def piece(i):
+def settle(source, target, held, fetched, kept):
+    count = kept.shape[0]
+    chunks = source.shape[0]
+    height = source.shape[1] // count
+
+    def fetch(i, chunk):
         rows = pl.ds(i * height, height)
-        return pltpu.make_async_copy(source.at[rows, :], target.at[rows, :], copied.at[i])
+        lanes = pl.ds(chunk * BLOCK, BLOCK)
+        return pltpu.make_async_copy(
+            source.at[chunk, rows, :], held.at[rows, lanes], fetched.at[i, chunk]
+        )
+
+    def keep(i):
+        rows = pl.ds(i * height, height)
+        return pltpu.make_async_copy(held.at[rows, :], target.at[rows, :], kept.at[i])
 
     for i in range(count):
-        piece(i).start()
+        for chunk in range(chunks):
+            fetch(i, chunk).start()
     for i in range(count):
-        piece(i).wait()
+        for chunk in range(chunks):
+            fetch(i, chunk).wait()
+        keep(i).start()
+    for i in range(count):
+        keep(i).wait()
 
 
 def fused(
@@ -271,7 +284,7 @@
         source = lax.rem(me + owners - by, owners)
         return pltpu.make_async_copy(
             early_staged.at[by],
-            out.at[pl.ds(pl.multiple_of(source * channels, 16), early_channels), :BLOCK],
+            out.at[0, pl.ds(pl.multiple_of(source * channels, 16), early_channels), :],
             early_kept.at[by],
         )
 
@@ -326,8 +339,7 @@
 
     def place(chunk, owner, first):
         return out.at[
-            pl.ds(pl.multiple_of(owner * channels + first, 16), channels - first),
-            chunk * BLOCK : (chunk + 1) * BLOCK,
+            chunk, pl.ds(pl.multiple_of(owner * channels + first, 16), channels - first), :
         ]
 
     def first_of(chunk):
@@ -417,7 +429,7 @@
     chunks = own // BLOCK
     later = max(chunks - 1, 1)
     devices = owners * across
-    at_once = next(n for n in (4, 2, 1) if groups % n == 0)
+    at_once = next(n for n in (2, 1) if groups % n == 0)
     steps = groups // at_once
     early_steps = steps // 2
     early_channels = max(early_steps, 1) * at_once * width
@@ -429,7 +441,7 @@
         functools.partial(fused, total_channels, at_once, early_steps),
         in_specs=[pl.BlockSpec(memory_space=pltpu.HBM)] + [pl.BlockSpec(memory_space=vmem)] * 5,
         out_specs=pl.BlockSpec(memory_space=pl.ANY),
-        out_shape=jax.ShapeDtypeStruct((owners * channels, own), bf16),
+        out_shape=jax.ShapeDtypeStruct((chunks, owners * channels, BLOCK), bf16),
         scratch_shapes=[
             vmem(streams.shape, bf16),
             vmem((chunks, owners, channels, BLOCK), f32),
@@ -467,8 +479,12 @@
         settle,
         in_specs=[pl.BlockSpec(memory_space=pl.ANY)],
         out_specs=pl.BlockSpec(memory_space=pl.ANY),
-        out_shape=jax.ShapeDtypeStruct(moved.shape, moved.dtype),
-        scratch_shapes=[dma((8,))],
+        out_shape=jax.ShapeDtypeStruct((owners * channels, own), bf16),
+        scratch_shapes=[
+            vmem((owners * channels, own), bf16),
+            dma((4, chunks)),
+            dma((4,)),
+        ],
         compiler_params=pltpu.CompilerParams(vmem_limit_bytes=56 * 1024 * 1024),
     )(moved)
 

time: 77.6 us -> 45.8 us (0.59)
  Pallas kernels: 76.9 us -> 45.1 us
    pallas_call x1, Pallas kernels: 32.9 us -> 2.1 us  [shards(): pl.pallas_call(settle, in_specs=[pl.BlockSpec(memory_space=pl.ANY)], out_...]
    pallas_call x1, Pallas kernels: 43.9 us -> 43 us  [shards(): pl.pallas_call(functools.partial(fused, total_channels, at_once, early_st...]
where the time goes in v6:
time: 45.8 us; the launch traced here: 45.2 us
  Pallas kernels  45.1 us (98%)
    pallas_call x1, Pallas kernels, shards(): pl.pallas_call(functools.partial(fused, total_channels, at_once, early_st...  43 us
    pallas_call x1, Pallas kernels, shards(): pl.pallas_call(settle, in_specs=[pl.BlockSpec(memory_space=pl.ANY)], out_...  2.1 us

profile of v6, /device:TPU:10, one launch (start us, length us, event | category | flops | bytes accessed | tf_op | source)
XLA Modules:
  0.0 45.2 jit_solution(17567816385528715691)
XLA Ops:
  0.0 43.0 %shard_map.64.source = bf16[2,2048,128]{2,1,0:T(8,128)(2,1)} custom-call(bf16[3,256,2048]{2,1,0:T(8,128)(2,1)} %streams.1, f32[3,7,128]{2,1,0:T(8,128)} %bitcast.5, f32[16,128]{1,0:T(8,128)} %bitcast.6, f32[16,128]{1,0:T(8,128)} %bitcast.7, f32[16,128]{1,0:T(8,128)} %bitcast.8, f32[16,128]{1,0:T(8,128)} %bitcast.9), custom_call_target="tpu_custom_call" | custom-call | tf_op jit(solution)/shard_map/pallas_call | solution.py:440
  43.1 2.1 %shard_map.65 = bf16[2048,256]{1,0:T(8,128)(2,1)} custom-call(bf16[2,2048,128]{2,1,0:T(8,128)(2,1)} %shard_map.64.source), custom_call_target="tpu_custom_call" | custom-call | tf_op jit(solution)/shard_map/pallas_call | solution.py:478

commit v7 on v6

--- a/solution.py
+++ b/solution.py
@@ -115,6 +115,9 @@
     gated_at,
     filters,
     tables,
+    backs,
+    columns,
+    states_at,
     held_at,
     squares,
     sums,
@@ -177,42 +180,41 @@
         at = (first_group + group) * width
         return upright(values[pl.ds(lax.div(at, BLOCK), 1), :], lax.rem(at, BLOCK), width)
 
-    def finish(group, chunk, held):
+    def finish(group, chunk):
         chosen = range(chunk, blocks, chunks)
-        value = short_filtered(window, 0, rows_of(group), chosen, filters[group])
-        high, low, starts = (held[:, i * BLOCK : (i + 1) * BLOCK] for i in range(3))
+        value = short_filtered(window, 0, rows_of(group), chosen, filters[0, group])
+        high, low, starts = (
+            held_at[chunk, group, :, i * BLOCK : (i + 1) * BLOCK] for i in range(3)
+        )
         convolved = jnp.dot(
             jnp.concatenate([high, low, high, starts], axis=1),
             tables[group],
             preferred_element_type=jnp.float32,
         )
-        skip = per_channel(skips, group)
-        gain = per_channel(gains, group)
         shaped = (owners, width, BLOCK)
         product = (high.astype(jnp.float32) + low.astype(jnp.float32)).reshape(shaped)
-        gated = value.reshape(shaped) * (convolved.reshape(shaped) + skip[None] * product)
-        gated_at[chunk, :, rows_of(group), :] = gated * gain[None]
+        gated = value.reshape(shaped) * (
+            convolved.reshape(shaped) + columns[1, group][None] * product
+        )
+        gated_at[chunk, :, rows_of(group), :] = gated * columns[2, group][None]
         return jnp.sum((gated * gated).reshape(owners, width // 8, 8, BLOCK), axis=1)
 
-    def begin(group):
+    spare = BLOCK - 3 * width
+
+    def tabulate(group):
         at = first_group + group
-        filters[group] = short_weights(picked(taps[0], at), causal)
-        product = 1.0
-        for m in (1, 2):
-            product *= short_filtered(
-                window, m, rows_of(group), range(blocks), short_weights(picked(taps[m], at), causal)
-            )
-        high, low = split(product)
-        pair = jnp.concatenate([high, low], axis=1)
-
-        rates = picked(pole_rates[...], at)
+        for m in range(3):
+            filters[m, group] = short_weights(picked(taps[m], at), causal)
+        rates = jnp.broadcast_to(picked(pole_rates[...], at), (width, BLOCK))
         residues = picked(residues_of[...], at)
+        columns[0, group] = rates
+        columns[1, group] = jnp.broadcast_to(per_channel(skips, group), (width, BLOCK))
+        columns[2, group] = jnp.broadcast_to(per_channel(gains, group), (width, BLOCK))
         lags = lax.broadcasted_iota(jnp.int32, (width, BLOCK), 1).astype(jnp.float32)
         modes = residues * jnp.exp(-rates * lags)
         table_high, table_low = split(rolled(jnp.sum(modes, axis=0, keepdims=True)))
         table_high = table_high * causal
         lift_high, lift_low = split(residues * jnp.exp(-rates * (lags + 1.0)))
-        spare = BLOCK - 3 * width
         tables[group] = jnp.concatenate(
             [
                 table_high,
@@ -225,47 +227,64 @@
             ],
             axis=0,
         )
-
         back_high, back_low = split(jnp.exp(-rates * (BLOCK - 1 - lags)))
-        back = jnp.concatenate(
+        backs[group] = jnp.concatenate(
             [
                 jnp.concatenate([back_high, back_high], axis=1),
                 jnp.concatenate([back_low, back_low], axis=1),
             ],
             axis=0,
         )
+
+    def keep_held(group, array, lanes):
+        for chunk in range(chunks):
+            held_at[chunk, group, :, lanes] = jnp.concatenate(
+                [array[n * width : (n + 1) * width] for n in range(chunk, blocks, chunks)], axis=0
+            )
+
+    def multiply(group):
+        product = 1.0
+        for m in (1, 2):
+            product *= short_filtered(
+                window, m, rows_of(group), range(blocks), filters[m, group]
+            )
+        high, low = split(product)
+        pair = jnp.concatenate([high, low], axis=1)
+        keep_held(group, pair, slice(0, 2 * BLOCK))
         ends = lax.dot_general(
-            back, pair, (((1,), (1,)), ((), ())), preferred_element_type=jnp.float32
-        )
-        states = ends[:width] + ends[width:]
-        lane = lax.broadcasted_iota(jnp.int32, states.shape, 1)
+            backs[group], pair, (((1,), (1,)), ((), ())), preferred_element_type=jnp.float32
+        )
+        states_at[group] = ends[:width] + ends[width:]
+
+    def scan(some):
+        shape = states_at.shape[1:]
+        lane = lax.broadcasted_iota(jnp.int32, shape, 1)
+        states = [states_at[group] for group in some]
+        rates = [columns[0, group] for group in some]
         reach = 1
         while reach < blocks:
-            earlier = pltpu.roll(states, reach * width, 1)
-            decay = jnp.exp(-rates * (BLOCK * reach))
-            states = states + jnp.where(lane >= reach * width, decay * earlier, 0.0)
+            earlier = [pltpu.roll(state, reach * width, 1) for state in states]
+            decays = [jnp.exp(-rate * (BLOCK * reach)) for rate in rates]
+            repeats = shape[1] // BLOCK
+            states = [
+                state
+                + jnp.where(
+                    lane >= reach * width, jnp.concatenate([decay] * repeats, axis=1) * before, 0.0
+                )
+                for state, decay, before in zip(states, decays, earlier)
+            ]
             reach *= 2
-        starts = jnp.where(lane >= width, pltpu.roll(states, width, 1), 0.0)
-        starts_high, starts_low = (part.astype(jnp.float32) for part in split(starts))
-        starts = jnp.concatenate(
-            [
+        for group, state in zip(some, states):
+            starts = jnp.where(lane >= width, pltpu.roll(state, width, 1), 0.0)
+            starts_high, starts_low = (part.astype(jnp.float32) for part in split(starts))
+            parts = [
                 starts_high,
                 starts_low,
                 starts_high,
-                jnp.zeros((spare, starts.shape[1]), jnp.float32),
-            ],
-            axis=0,
-        ).T.astype(jnp.bfloat16)
-        held = jnp.concatenate([pair, starts], axis=1)
-
-        def of_chunk(chunk):
-            return jnp.concatenate(
-                [held[n * width : (n + 1) * width] for n in range(chunk, blocks, chunks)], axis=0
-            )
-
-        for chunk in range(1, chunks):
-            held_at[chunk - 1, group] = of_chunk(chunk)
-        return of_chunk(0)
+                jnp.zeros((spare, shape[1]), jnp.float32),
+            ]
+            upended = jnp.concatenate(parts, axis=0).T.astype(jnp.bfloat16)
+            keep_held(group, upended, slice(2 * BLOCK, 3 * BLOCK))
 
     early_channels = early_steps * at_once * width
 
@@ -301,10 +320,24 @@
 
     @pl.loop(0, steps)
     def _(step):
+        for i in range(at_once):
+            tabulate(step * at_once + i)
+
+    @pl.loop(0, steps)
+    def _(step):
         fetch(step).wait()
-        begun = [begin(step * at_once + i) for i in range(at_once)]
-        for i, held in enumerate(begun):
-            squares[0] += finish(step * at_once + i, 0, held)
+        for i in range(at_once):
+            multiply(step * at_once + i)
+
+    abreast = next(n for n in (8, 4, 2, 1) if groups % n == 0)
+
+    @pl.loop(0, groups // abreast)
+    def _(step):
+        scan([step * abreast + i for i in range(abreast)])
+
+    @pl.loop(0, steps)
+    def _(step):
+        squares[0] += sum(finish(step * at_once + i, 0) for i in range(at_once))
 
         if early_steps:
 
@@ -321,11 +354,7 @@
     def later(chunk, low, high):
         @pl.loop(low, high)
         def _(step):
-            total = 0.0
-            for i in range(at_once):
-                group = step * at_once + i
-                total += finish(group, chunk, held_at[chunk - 1, group])
-            squares[chunk] += total
+            squares[chunk] += sum(finish(step * at_once + i, chunk) for i in range(at_once))
 
     def sums_copy(chunk, by):
         return pltpu.make_async_remote_copy(
@@ -427,11 +456,10 @@
     assert pole_rates.shape[1] == width
     own = length // owners
     chunks = own // BLOCK
-    later = max(chunks - 1, 1)
     devices = owners * across
-    at_once = next(n for n in (2, 1) if groups % n == 0)
+    at_once = next(n for n in (4, 2, 1) if groups % n == 0)
     steps = groups // at_once
-    early_steps = steps // 2
+    early_steps = steps // 4
     early_channels = max(early_steps, 1) * at_once * width
     vmem = pltpu.VMEM
     dma = pltpu.SemaphoreType.DMA
@@ -445,9 +473,12 @@
         scratch_shapes=[
             vmem(streams.shape, bf16),
             vmem((chunks, owners, channels, BLOCK), f32),
-            vmem((groups, 2 * BLOCK, 2 * BLOCK), bf16),
+            vmem((3, groups, 2 * BLOCK, 2 * BLOCK), bf16),
             vmem((groups, 4 * BLOCK, BLOCK), bf16),
-            vmem((later, groups, owners * width, 3 * BLOCK), bf16),
+            vmem((groups, 2 * width, 2 * BLOCK), bf16),
+            vmem((3, groups, width, BLOCK), f32),
+            vmem((groups, width, length // BLOCK * width), f32),
+            vmem((chunks, groups, owners * width, 3 * BLOCK), bf16),
             vmem((chunks, owners, 8, BLOCK), f32),
             vmem((chunks, devices, owners, BLOCK), f32),
             vmem((chunks, owners, BLOCK), f32),

time: 45.8 us -> 53.2 us (1.16)
  Pallas kernels: 45.1 us -> 52.3 us
    pallas_call x1, Pallas kernels: 43 us -> 50.2 us  [shards(): pl.pallas_call(functools.partial(fused, total_channels, at_once, early_st...]
where the time goes in v7:
time: 53.2 us; the launch traced here: 52.3 us
  Pallas kernels  52.3 us (98%)
    pallas_call x1, Pallas kernels, shards(): pl.pallas_call(functools.partial(fused, total_channels, at_once, early_st...  50.2 us
    pallas_call x1, Pallas kernels, shards(): pl.pallas_call(settle, in_specs=[pl.BlockSpec(memory_space=pl.ANY)], out_...  2.1 us

profile of v7, /device:TPU:10, one launch (start us, length us, event | category | flops | bytes accessed | tf_op | source)
XLA Modules:
  0.0 52.3 jit_solution(13115825430147151487)
XLA Ops:
  0.0 50.2 %shard_map.64.source = bf16[2,2048,128]{2,1,0:T(8,128)(2,1)} custom-call(bf16[3,256,2048]{2,1,0:T(8,128)(2,1)} %streams.1, f32[3,7,128]{2,1,0:T(8,128)} %bitcast.5, f32[16,128]{1,0:T(8,128)} %bitcast.6, f32[16,128]{1,0:T(8,128)} %bitcast.7, f32[16,128]{1,0:T(8,128)} %bitcast.8, f32[16,128]{1,0:T(8,128)} %bitcast.9), custom_call_target="tpu_custom_call" | custom-call | tf_op jit(solution)/shard_map/pallas_call | solution.py:468
  50.2 2.1 %shard_map.65 = bf16[2048,256]{1,0:T(8,128)(2,1)} custom-call(bf16[2,2048,128]{2,1,0:T(8,128)(2,1)} %shard_map.64.source), custom_call_target="tpu_custom_call" | custom-call | tf_op jit(solution)/shard_map/pallas_call | solution.py:509

commit v8 on v6

--- a/solution.py
+++ b/solution.py
@@ -22,8 +22,9 @@
 
 
 def rolled(row):
-    return pltpu.roll(
-        jnp.broadcast_to(row, (BLOCK, BLOCK)), 0, 1, stride=1, stride_axis=0
+    tile = pltpu.roll(jnp.broadcast_to(row, (8, BLOCK)), 0, 1, stride=1, stride_axis=0)
+    return jnp.concatenate(
+        [tile] + [pltpu.roll(tile, turn, 1) for turn in range(8, BLOCK, 8)], axis=0
     )
 
 

time: 45.8 us -> 45.7 us (level)
  no operation moved by 1% of the time
where the time goes in v8:
time: 45.7 us; the launch traced here: 45.2 us
  Pallas kernels  45.1 us (99%)
    pallas_call x1, Pallas kernels, shards(): pl.pallas_call(functools.partial(fused, total_channels, at_once, early_st...  43 us
    pallas_call x1, Pallas kernels, shards(): pl.pallas_call(settle, in_specs=[pl.BlockSpec(memory_space=pl.ANY)], out_...  2.1 us

profile of v8, /device:TPU:10, one launch (start us, length us, event | category | flops | bytes accessed | tf_op | source)
XLA Modules:
  0.0 45.2 jit_solution(13868506322124239874)
XLA Ops:
  0.0 43.0 %shard_map.64.source = bf16[2,2048,128]{2,1,0:T(8,128)(2,1)} custom-call(bf16[3,256,2048]{2,1,0:T(8,128)(2,1)} %streams.1, f32[3,7,128]{2,1,0:T(8,128)} %bitcast.5, f32[16,128]{1,0:T(8,128)} %bitcast.6, f32[16,128]{1,0:T(8,128)} %bitcast.7, f32[16,128]{1,0:T(8,128)} %bitcast.8, f32[16,128]{1,0:T(8,128)} %bitcast.9), custom_call_target="tpu_custom_call" | custom-call | tf_op jit(solution)/shard_map/pallas_call | solution.py:441
  43.1 2.1 %shard_map.65 = bf16[2048,256]{1,0:T(8,128)(2,1)} custom-call(bf16[2,2048,128]{2,1,0:T(8,128)(2,1)} %shard_map.64.source), custom_call_target="tpu_custom_call" | custom-call | tf_op jit(solution)/shard_map/pallas_call | solution.py:479

commit v9 on v8

--- a/solution.py
+++ b/solution.py
@@ -118,7 +118,9 @@
     tables,
     held_at,
     squares,
-    sums,
+    across,
+    column,
+    along,
     scales,
     staged,
     early,
@@ -127,8 +129,10 @@
     early_sent,
     early_got,
     early_kept,
-    sums_sent,
-    sums_got,
+    across_sent,
+    across_got,
+    along_sent,
+    along_got,
     block_sent,
     block_got,
     kept,
@@ -153,21 +157,34 @@
     def _(step):
         fetch(step).start()
 
+    def partner(by):
+        result = 0
+        bit = 1
+        while bit < owners:
+            mine, its = lax.rem(lax.div(me, bit), 2), lax.rem(lax.div(by, bit), 2)
+            result = result + bit * (mine + its - 2 * mine * its)
+            bit *= 2
+        return result
+
+    def far_first(i):
+        return owners - i
+
     def peer_ctx(by):
-        return {"ctx": lax.rem(me + by, owners)}
-
-    def peer(by):
-        return {
-            "ctx": lax.rem(me + lax.div(by, across_count), owners),
-            "ch": lax.rem(my_ch + lax.rem(by, across_count), across_count),
-        }
-
-    devices = owners * across_count
+        return {"ctx": partner(by)}
+
+    def peer_ch(by):
+        return {"ch": lax.rem(my_ch + by, across_count)}
+
+    greeted = across_count + owners - 2
     barrier = pltpu.get_barrier_semaphore()
 
-    @pl.loop(1, devices)
+    @pl.loop(1, across_count)
     def _(by):
-        pl.semaphore_signal(barrier, inc=1, device_id=peer(by), device_id_type=MESH)
+        pl.semaphore_signal(barrier, inc=1, device_id=peer_ch(by), device_id_type=MESH)
+
+    @pl.loop(1, owners)
+    def _(by):
+        pl.semaphore_signal(barrier, inc=1, device_id=peer_ctx(by), device_id_type=MESH)
 
     causal = causal_mask()
 
@@ -273,7 +290,7 @@
     def early_copy(step, by):
         rows = pl.ds(pl.multiple_of(step * (at_once * width), 16), at_once * width)
         return pltpu.make_async_remote_copy(
-            src_ref=gated_at.at[0, lax.rem(me + by, owners), rows, :],
+            src_ref=gated_at.at[0, partner(by), rows, :],
             dst_ref=early.at[by, rows, :],
             send_sem=early_sent.at[step, by],
             recv_sem=early_got.at[step, by],
@@ -282,7 +299,7 @@
         )
 
     def early_keep(by):
-        source = lax.rem(me + owners - by, owners)
+        source = partner(by)
         return pltpu.make_async_copy(
             early_staged.at[by],
             out.at[0, pl.ds(pl.multiple_of(source * channels, 16), early_channels), :],
@@ -311,13 +328,13 @@
 
             @pl.when(step == 0)
             def _():
-                pl.semaphore_wait(barrier, devices - 1)
+                pl.semaphore_wait(barrier, greeted)
 
             @pl.when(step < early_steps)
             def _():
                 @pl.loop(1, owners)
-                def _(by):
-                    early_copy(step, by).start()
+                def _(i):
+                    early_copy(step, far_first(i)).start()
 
     def later(chunk, low, high):
         @pl.loop(low, high)
@@ -328,13 +345,23 @@
                 total += finish(group, chunk, held_at[chunk - 1, group])
             squares[chunk] += total
 
-    def sums_copy(chunk, by):
+    def across_copy(chunk, by):
         return pltpu.make_async_remote_copy(
-            src_ref=sums.at[chunk, 0],
-            dst_ref=sums.at[chunk, by],
-            send_sem=sums_sent.at[chunk, by],
-            recv_sem=sums_got.at[chunk, by],
-            device_id=peer(by),
+            src_ref=across.at[chunk, 0],
+            dst_ref=across.at[chunk, by],
+            send_sem=across_sent.at[chunk, by],
+            recv_sem=across_got.at[chunk, by],
+            device_id=peer_ch(by),
+            device_id_type=MESH,
+        )
+
+    def along_copy(chunk, by):
+        return pltpu.make_async_remote_copy(
+            src_ref=column.at[chunk],
+            dst_ref=along.at[chunk, by],
+            send_sem=along_sent.at[chunk, by],
+            recv_sem=along_got.at[chunk, by],
+            device_id=peer_ctx(by),
             device_id_type=MESH,
         )
 
@@ -362,23 +389,36 @@
             staged.at[chunk, 0], place(chunk, me, 0), kept.at[chunk]
         )
 
-    def start_sums(chunk):
-        sums[chunk, 0] = jnp.sum(squares[chunk], axis=1)
-
-        @pl.loop(1, devices)
-        def _(by):
-            sums_copy(chunk, by).start()
-
-    def start_blocks(chunk):
-        @pl.loop(1, devices)
-        def _(by):
-            sums_copy(chunk, by).wait()
-
-        total = jnp.sum(sums[chunk], axis=0)
+    def start_across(chunk):
+        across[chunk, 0] = jnp.sum(squares[chunk], axis=1)
+
+        @pl.loop(1, across_count)
+        def _(by):
+            across_copy(chunk, by).start()
+
+    def start_along(chunk):
+        @pl.loop(1, across_count)
+        def _(by):
+            across_copy(chunk, by).wait()
+
+        column[chunk] = jnp.sum(across[chunk], axis=0)
+
+        @pl.loop(1, owners)
+        def _(i):
+            along_copy(chunk, far_first(i)).start()
+
+    def fill_blocks(chunk):
+        along[chunk, 0] = column[chunk]
+
+        @pl.loop(1, owners)
+        def _(by):
+            along_copy(chunk, by).wait()
+
+        total = jnp.sum(along[chunk], axis=0)
         scales[chunk] = lax.rsqrt(total / total_channels + 1e-05)
 
         def fill(by, first):
-            target = lax.rem(me + by, owners)
+            target = partner(by)
             row = scales[chunk, pl.ds(target, 1), :]
             staged[chunk, by, first:, :] = (gated_at[chunk, target, first:, :] * row).astype(
                 jnp.bfloat16
@@ -387,26 +427,38 @@
         @pl.loop(1, owners)
         def _(by):
             fill(by, first_of(chunk))
-            block_copy(chunk, by, me).start()
 
         fill(0, 0)
         own_copy(chunk).start()
 
+    def start_blocks(chunk):
+        @pl.loop(1, owners)
+        def _(i):
+            block_copy(chunk, far_first(i), me).start()
+
     def wait_blocks(chunk):
         own_copy(chunk).wait()
 
         @pl.loop(1, owners)
         def _(by):
             block_copy(chunk, by, me).wait_send()
-            block_copy(chunk, by, lax.rem(me + owners - by, owners)).wait_recv()
+            block_copy(chunk, by, partner(by)).wait_recv()
 
     if not early_steps:
-        pl.semaphore_wait(barrier, devices - 1)
-    start_sums(0)
+        pl.semaphore_wait(barrier, greeted)
+    start_across(0)
     for chunk in range(chunks):
-        if chunk + 1 < chunks:
-            later(chunk + 1, 0, steps)
-            start_sums(chunk + 1)
+        more = chunk + 1 < chunks
+        if more and chunk == 0:
+            later(1, 0, steps // 2)
+        if chunk == 0:
+            start_along(0)
+        if more:
+            later(chunk + 1, steps // 2 if chunk == 0 else 0, steps)
+            start_across(chunk + 1)
+        fill_blocks(chunk)
+        if more:
+            start_along(chunk + 1)
         start_blocks(chunk)
     if early_steps:
         keep_early()
@@ -429,7 +481,6 @@
     own = length // owners
     chunks = own // BLOCK
     later = max(chunks - 1, 1)
-    devices = owners * across
     at_once = next(n for n in (2, 1) if groups % n == 0)
     steps = groups // at_once
     early_steps = steps // 2
@@ -450,7 +501,9 @@
             vmem((groups, 4 * BLOCK, BLOCK), bf16),
             vmem((later, groups, owners * width, 3 * BLOCK), bf16),
             vmem((chunks, owners, 8, BLOCK), f32),
-            vmem((chunks, devices, owners, BLOCK), f32),
+            vmem((chunks, across, owners, BLOCK), f32),
+            vmem((chunks, owners, BLOCK), f32),
+            vmem((chunks, owners, owners, BLOCK), f32),
             vmem((chunks, owners, BLOCK), f32),
             vmem((chunks, owners, channels, BLOCK), bf16),
             vmem((owners, early_channels, BLOCK), f32),
@@ -459,8 +512,10 @@
             dma((max(early_steps, 1), owners)),
             dma((max(early_steps, 1), owners)),
             dma((owners,)),
-            dma((chunks, devices)),
-            dma((chunks, devices)),
+            dma((chunks, across)),
+            dma((chunks, across)),
+            dma((chunks, owners)),
+            dma((chunks, owners)),
             dma((chunks, owners)),
             dma((chunks, owners)),
             dma((chunks,)),

time: 45.7 us -> 47.4 us (1.037)
  the two profiles are of different devices: /device:TPU:10 before, /device:TPU:0 now
where the time goes in v9:
time: 47.4 us; the launch traced here: 47.2 us
  Pallas kernels  47.2 us (100%)
    pallas_call x1, Pallas kernels, shards(): pl.pallas_call(functools.partial(fused, total_channels, at_once, early_st...  45.1 us
    pallas_call x1, Pallas kernels, shards(): pl.pallas_call(settle, in_specs=[pl.BlockSpec(memory_space=pl.ANY)], out_...  2.1 us

profile of v9, /device:TPU:0, one launch (start us, length us, event | category | flops | bytes accessed | tf_op | source)
XLA Modules:
  0.0 47.2 jit_solution(4489095935527490291)
XLA Ops:
  0.0 45.1 %shard_map.64.source = bf16[2,2048,128]{2,1,0:T(8,128)(2,1)} custom-call(bf16[3,256,2048]{2,1,0:T(8,128)(2,1)} %streams.1, f32[3,7,128]{2,1,0:T(8,128)} %bitcast.5, f32[16,128]{1,0:T(8,128)} %bitcast.6, f32[16,128]{1,0:T(8,128)} %bitcast.7, f32[16,128]{1,0:T(8,128)} %bitcast.8, f32[16,128]{1,0:T(8,128)} %bitcast.9), custom_call_target="tpu_custom_call" | custom-call | tf_op jit(solution)/shard_map/pallas_call | solution.py:492
  45.1 2.1 %shard_map.65 = bf16[2048,256]{1,0:T(8,128)(2,1)} custom-call(bf16[2,2048,128]{2,1,0:T(8,128)(2,1)} %shard_map.64.source), custom_call_target="tpu_custom_call" | custom-call | tf_op jit(solution)/shard_map/pallas_call | solution.py:534

commit v10 on v9

--- a/solution.py
+++ b/solution.py
@@ -407,7 +407,7 @@
         def _(i):
             along_copy(chunk, far_first(i)).start()
 
-    def fill_blocks(chunk):
+    def send_blocks(chunk, meanwhile):
         along[chunk, 0] = column[chunk]
 
         @pl.loop(1, owners)
@@ -424,17 +424,17 @@
                 jnp.bfloat16
             )
 
-        @pl.loop(1, owners)
-        def _(by):
+        def send(i):
+            by = far_first(i)
             fill(by, first_of(chunk))
-
+            block_copy(chunk, by, me).start()
+
+        cut = min(4, owners)
+        pl.loop(1, cut)(send)
+        meanwhile()
+        pl.loop(cut, owners)(send)
         fill(0, 0)
         own_copy(chunk).start()
-
-    def start_blocks(chunk):
-        @pl.loop(1, owners)
-        def _(i):
-            block_copy(chunk, far_first(i), me).start()
 
     def wait_blocks(chunk):
         own_copy(chunk).wait()
@@ -456,10 +456,7 @@
         if more:
             later(chunk + 1, steps // 2 if chunk == 0 else 0, steps)
             start_across(chunk + 1)
-        fill_blocks(chunk)
-        if more:
-            start_along(chunk + 1)
-        start_blocks(chunk)
+        send_blocks(chunk, functools.partial(start_along, chunk + 1) if more else lambda: None)
     if early_steps:
         keep_early()
     for chunk in range(chunks):
@@ -479,11 +476,12 @@
     width = channels // groups
     assert pole_rates.shape[1] == width
     own = length // owners
+    assert owners & (owners - 1) == 0
     chunks = own // BLOCK
     later = max(chunks - 1, 1)
     at_once = next(n for n in (2, 1) if groups % n == 0)
     steps = groups // at_once
-    early_steps = steps // 2
+    early_steps = 3 * steps // 8
     early_channels = max(early_steps, 1) * at_once * width
     vmem = pltpu.VMEM
     dma = pltpu.SemaphoreType.DMA

time: 47.4 us -> 48.4 us (1.021)
  Pallas kernels: 47.2 us -> 48.1 us
    pallas_call x1, Pallas kernels: 45.1 us -> 46 us  [shards(): pl.pallas_call(functools.partial(fused, total_channels, at_once, early_st...]
where the time goes in v10:
time: 48.4 us; the launch traced here: 48.1 us
  Pallas kernels  48.1 us (99%)
    pallas_call x1, Pallas kernels, shards(): pl.pallas_call(functools.partial(fused, total_channels, at_once, early_st...  46 us
    pallas_call x1, Pallas kernels, shards(): pl.pallas_call(settle, in_specs=[pl.BlockSpec(memory_space=pl.ANY)], out_...  2.1 us

profile of v10, /device:TPU:0, one launch (start us, length us, event | category | flops | bytes accessed | tf_op | source)
XLA Modules:
  0.0 48.1 jit_solution(5744477024815755880)
XLA Ops:
  0.0 46.0 %shard_map.64.source = bf16[2,2048,128]{2,1,0:T(8,128)(2,1)} custom-call(bf16[3,256,2048]{2,1,0:T(8,128)(2,1)} %streams.1, f32[3,7,128]{2,1,0:T(8,128)} %bitcast.5, f32[16,128]{1,0:T(8,128)} %bitcast.6, f32[16,128]{1,0:T(8,128)} %bitcast.7, f32[16,128]{1,0:T(8,128)} %bitcast.8, f32[16,128]{1,0:T(8,128)} %bitcast.9), custom_call_target="tpu_custom_call" | custom-call | tf_op jit(solution)/shard_map/pallas_call | solution.py:490
  46.0 2.1 %shard_map.65 = bf16[2048,256]{1,0:T(8,128)(2,1)} custom-call(bf16[2,2048,128]{2,1,0:T(8,128)(2,1)} %shard_map.64.source), custom_call_target="tpu_custom_call" | custom-call | tf_op jit(solution)/shard_map/pallas_call | solution.py:532

commit v11 on v8

--- a/solution.py
+++ b/solution.py
@@ -432,7 +432,7 @@
     devices = owners * across
     at_once = next(n for n in (2, 1) if groups % n == 0)
     steps = groups // at_once
-    early_steps = steps // 2
+    early_steps = 3 * steps // 4
     early_channels = max(early_steps, 1) * at_once * width
     vmem = pltpu.VMEM
     dma = pltpu.SemaphoreType.DMA

time: 45.7 us -> 49 us (1.072)
  Pallas kernels: 45.1 us -> 48.6 us
    pallas_call x1, Pallas kernels: 43 us -> 46.5 us  [shards(): pl.pallas_call(functools.partial(fused, total_channels, at_once, early_st...]
where the time goes in v11:
time: 49 us; the launch traced here: 48.6 us
  Pallas kernels  48.6 us (99%)
    pallas_call x1, Pallas kernels, shards(): pl.pallas_call(functools.partial(fused, total_channels, at_once, early_st...  46.5 us
    pallas_call x1, Pallas kernels, shards(): pl.pallas_call(settle, in_specs=[pl.BlockSpec(memory_space=pl.ANY)], out_...  2.1 us

profile of v11, /device:TPU:10, one launch (start us, length us, event | category | flops | bytes accessed | tf_op | source)
XLA Modules:
  0.0 48.6 jit_solution(2970651462362284920)
XLA Ops:
  0.0 46.5 %shard_map.64.source = bf16[2,2048,128]{2,1,0:T(8,128)(2,1)} custom-call(bf16[3,256,2048]{2,1,0:T(8,128)(2,1)} %streams.1, f32[3,7,128]{2,1,0:T(8,128)} %bitcast.5, f32[16,128]{1,0:T(8,128)} %bitcast.6, f32[16,128]{1,0:T(8,128)} %bitcast.7, f32[16,128]{1,0:T(8,128)} %bitcast.8, f32[16,128]{1,0:T(8,128)} %bitcast.9), custom_call_target="tpu_custom_call" | custom-call | tf_op jit(solution)/shard_map/pallas_call | solution.py:441
  46.5 2.1 %shard_map.65 = bf16[2048,256]{1,0:T(8,128)(2,1)} custom-call(bf16[2,2048,128]{2,1,0:T(8,128)(2,1)} %shard_map.64.source), custom_call_target="tpu_custom_call" | custom-call | tf_op jit(solution)/shard_map/pallas_call | solution.py:479

commit v12 on v11

--- a/solution.py
+++ b/solution.py
@@ -432,7 +432,7 @@
     devices = owners * across
     at_once = next(n for n in (2, 1) if groups % n == 0)
     steps = groups // at_once
-    early_steps = 3 * steps // 4
+    early_steps = 3 * steps // 8
     early_channels = max(early_steps, 1) * at_once * width
     vmem = pltpu.VMEM
     dma = pltpu.SemaphoreType.DMA

time: 49 us -> 46.3 us (0.945)
  Pallas kernels: 48.6 us -> 45.8 us
    pallas_call x1, Pallas kernels: 46.5 us -> 43.7 us  [shards(): pl.pallas_call(functools.partial(fused, total_channels, at_once, early_st...]
where the time goes in v12:
time: 46.3 us; the launch traced here: 45.9 us
  Pallas kernels  45.8 us (99%)
    pallas_call x1, Pallas kernels, shards(): pl.pallas_call(functools.partial(fused, total_channels, at_once, early_st...  43.7 us
    pallas_call x1, Pallas kernels, shards(): pl.pallas_call(settle, in_specs=[pl.BlockSpec(memory_space=pl.ANY)], out_...  2.1 us

profile of v12, /device:TPU:10, one launch (start us, length us, event | category | flops | bytes accessed | tf_op | source)
XLA Modules:
  0.0 45.9 jit_solution(11558056731137007252)
XLA Ops:
  0.0 43.7 %shard_map.64.source = bf16[2,2048,128]{2,1,0:T(8,128)(2,1)} custom-call(bf16[3,256,2048]{2,1,0:T(8,128)(2,1)} %streams.1, f32[3,7,128]{2,1,0:T(8,128)} %bitcast.5, f32[16,128]{1,0:T(8,128)} %bitcast.6, f32[16,128]{1,0:T(8,128)} %bitcast.7, f32[16,128]{1,0:T(8,128)} %bitcast.8, f32[16,128]{1,0:T(8,128)} %bitcast.9), custom_call_target="tpu_custom_call" | custom-call | tf_op jit(solution)/shard_map/pallas_call | solution.py:441
  43.8 2.1 %shard_map.65 = bf16[2048,256]{1,0:T(8,128)(2,1)} custom-call(bf16[2,2048,128]{2,1,0:T(8,128)(2,1)} %shard_map.64.source), custom_call_target="tpu_custom_call" | custom-call | tf_op jit(solution)/shard_map/pallas_call | solution.py:479
